TPU v7x, 512 devices: a whole 4x4x16 slice. The times are simulated.
512 devices in a mesh: tm: 64 (over x, z), strip: 8 (over y, core).
Axes of the slice: x: 4, y: 4, z: 16, core: 2. Of those that a mesh axis runs over, the one named last changes fastest.
Arguments:
- frames: bfloat16 [2048, 128, 2048], P('tm', None, 'strip'), may hold values from -16 to 16
- freqs: int32 [16], replicated, may hold values from 1 to 64
- valid: int32 [128, 2048], P('tm', 'strip'), may hold values 0 or 1
- classes: int32 [128, 2048], P('tm', 'strip'), may hold values from 0 to 3
Outputs:
- smoothed: float32 [3, 128, 2048], P(None, 'tm', 'strip')
All inputs are finite; a program needn't handle non-finite values. No bound on the sum of `valid` on one device may be relied on, other than what follows from the above.
Results may differ from a plain program's by a relative error of at most 0.00049.
Values may be sent and summed in bfloat16 or wider, within the bound.
No kernel may reach another device: no remote copies, remote signals or barrier semaphores. Data moves between devices by JAX's collectives and lax.ppermute only.
A program may use at most 64 MiB of HBM per device.

v0:
```python
import math

import jax
import jax.numpy as jnp
from jax import lax
from jax.sharding import PartitionSpec as P

TV_PASSES = 3


EPS_TV = 1.0
STEP_TV = 0.2


def with_halo(block, sides, width):
    for axis, dim in sides:
        count = lax.axis_size(axis)
        forward = [(i, i + 1) for i in range(count - 1)]
        backward = [(target, source) for source, target in forward]
        low = lax.ppermute(
            lax.slice_in_dim(block, block.shape[dim] - width, None, axis=dim), axis, forward
        )
        high = lax.ppermute(lax.slice_in_dim(block, 0, width, axis=dim), axis, backward)
        block = jnp.concatenate([low, block, high], axis=dim)
    return block


def angle_table(freqs, times, total):
    phase = freqs[:, None] * times[None, :] % total
    angle = phase.astype(jnp.float32) * (2.0 * math.pi / total)
    return jnp.concatenate([jnp.cos(angle), -jnp.sin(angle)], axis=0).astype(jnp.bfloat16)


def start_params(classes):
    level = classes.astype(jnp.float32)
    return jnp.stack([-0.3 + 0.2 * level, 0.5 - 0.3 * level, -0.5 + 0.25 * level])


def model_pieces(start, freqs):
    alpha_par, beta_par, gamma_par = (start[0], start[1], start[2])
    weight = jnp.sqrt(freqs.astype(jnp.float32) / 8.0)[:, None, None]
    amp = jnp.exp(alpha_par)
    tanh_b = jnp.tanh(beta_par)
    refl = 0.8 * tanh_b
    slope = 0.8 * (1.0 - tanh_b * tanh_b)
    depth = jnp.exp(gamma_par) * weight
    decay = jnp.exp(-2.0 * depth)
    e_re = decay * jnp.cos(2.0 * depth)
    e_im = -decay * jnp.sin(2.0 * depth)
    g_re = refl * e_re
    g_im = refl * e_im
    d_re = 1.0 - g_re
    d_im = -g_im
    denom = d_re * d_re + d_im * d_im
    q_re = ((1.0 + g_re) * d_re + g_im * d_im) / denom
    q_im = (g_im * d_re - (1.0 + g_re) * d_im) / denom
    scale = amp / (math.sqrt(2.0) * weight)

    def project(z_re, z_im):
        return (scale * (z_re + z_im), scale * (z_im - z_re))

    m_re, m_im = project(q_re, q_im)
    den_sq = denom * denom
    p_re = 2.0 * (d_re * d_re - d_im * d_im) / den_sq
    p_im = -4.0 * d_re * d_im / den_sq
    zb_re = (p_re * e_re - p_im * e_im) * slope
    zb_im = (p_re * e_im + p_im * e_re) * slope
    h_re = -2.0 * depth * (g_re - g_im)
    h_im = -2.0 * depth * (g_re + g_im)
    zc_re = p_re * h_re - p_im * h_im
    zc_im = p_re * h_im + p_im * h_re
    columns = [(m_re, m_im), project(zb_re, zb_im), project(zc_re, zc_im)]
    return (m_re, m_im, columns)


def solve_step(columns, rhs, start, valid):
    mat = [
        [
            jnp.sum(columns[i][0] * columns[j][0] + columns[i][1] * columns[j][1], axis=0)
            for j in range(3)
        ]
        for i in range(3)
    ]
    damping = 0.1 * (mat[0][0] + mat[1][1] + mat[2][2]) / 3.0 + 0.01
    a00 = mat[0][0] + damping
    a11 = mat[1][1] + damping
    a22 = mat[2][2] + damping
    a01 = mat[0][1]
    a02 = mat[0][2]
    a12 = mat[1][2]
    c00 = a11 * a22 - a12 * a12
    c01 = a02 * a12 - a01 * a22
    c02 = a01 * a12 - a02 * a11
    c11 = a00 * a22 - a02 * a02
    c12 = a01 * a02 - a00 * a12
    c22 = a00 * a11 - a01 * a01
    determinant = a00 * c00 + a01 * c01 + a02 * c02
    delta = jnp.stack(
        [
            (c00 * rhs[0] + c01 * rhs[1] + c02 * rhs[2]) / determinant,
            (c01 * rhs[0] + c11 * rhs[1] + c12 * rhs[2]) / determinant,
            (c02 * rhs[0] + c12 * rhs[1] + c22 * rhs[2]) / determinant,
        ]
    )
    return jnp.where(valid[None] == 1, start + delta, start)


def gauss_newton(y_re, y_im, start, freqs, valid):
    m_re, m_im, columns = model_pieces(start, freqs)
    res_re = y_re - m_re
    res_im = y_im - m_im
    rhs = [jnp.sum(columns[i][0] * res_re + columns[i][1] * res_im, axis=0) for i in range(3)]
    return solve_step(columns, rhs, start, valid)


def tv_pass(padded, field, fitted, row_first, col_first, rows_all, cols_all):
    rows_here = field.shape[1]
    cols_here = field.shape[2]
    grad_x = padded[:, 1:, : cols_here + 1] - padded[:, : rows_here + 1, : cols_here + 1]
    grad_y = padded[:, : rows_here + 1, 1:] - padded[:, : rows_here + 1, : cols_here + 1]
    row_ids = row_first - 1 + jnp.arange(rows_here + 1, dtype=jnp.int32)
    col_ids = col_first - 1 + jnp.arange(cols_here + 1, dtype=jnp.int32)
    row_good = (row_ids >= 0) & (row_ids <= rows_all - 2)
    col_good = (col_ids >= 0) & (col_ids <= cols_all - 2)
    grad_x = jnp.where(row_good[None, :, None], grad_x, jnp.float32(0.0))
    grad_y = jnp.where(col_good[None, None, :], grad_y, jnp.float32(0.0))
    length = jnp.sqrt(grad_x * grad_x + grad_y * grad_y + EPS_TV * EPS_TV)
    flux_x = grad_x / length
    flux_y = grad_y / length
    diverge = flux_x[:, 1:, 1:] - flux_x[:, :-1, 1:] + flux_y[:, 1:, 1:] - flux_y[:, 1:, :-1]
    return field + STEP_TV * (diverge - (field - fitted))


def on_device(frames, freqs, valid, classes):
    frame_count = frames.shape[0]
    time_devs = lax.axis_size("tm")
    strip_devs = lax.axis_size("strip")
    total_frames = frame_count * time_devs
    tile_rows = valid.shape[0]
    tile_cols = valid.shape[1]
    harmonics = freqs.shape[0]
    start = start_params(classes)
    times_here = lax.axis_index("tm") * frame_count + jnp.arange(frame_count, dtype=jnp.int32)
    table_here = angle_table(freqs, times_here, total_frames)
    spectrum = lax.psum_scatter(
        jnp.einsum("kt,trc->rkc", table_here, frames, preferred_element_type=jnp.float32),
        "tm",
        scatter_dimension=0,
        tiled=True,
    )
    spectrum = jnp.transpose(spectrum, (1, 0, 2)) / math.sqrt(total_frames)
    fitted = gauss_newton(spectrum[:harmonics], spectrum[harmonics:], start, freqs, valid)
    row_first = lax.axis_index("tm") * tile_rows
    col_first = lax.axis_index("strip") * tile_cols
    rows_all = tile_rows * time_devs
    cols_all = tile_cols * strip_devs
    field = fitted
    for step in range(TV_PASSES):
        padded = with_halo(field, (("tm", 1), ("strip", 2)), 1)
        field = tv_pass(padded, field, fitted, row_first, col_first, rows_all, cols_all)
    return field


def solution(mesh):
    placed = (P("tm", None, "strip"), P(), P("tm", "strip"), P("tm", "strip"))
    return jax.shard_map(
        on_device, mesh=mesh, in_specs=placed, out_specs=P(None, "tm", "strip"), check_vma=False
    )
```

profile of v0, /device:TPU:1, one launch (start us, length us, event | category | flops | bytes accessed | tf_op | source)
XLA Modules:
  0.0 776.2 jit_solution(746550068953636881)
XLA Ops:
  6.5 0.9 cosine_convert_fusion
  7.5 0.7 copy-done
  8.1 3.3 convolution_bitcast_fusion
  11.5 0.6 copy-done.3
  12.2 693.9 %reduce-scatter.2.cloned.1.call-done = f32[2,32,256]{2,1,0:T(8,128)} async-done(((f32[128,32,256]{2,1,0:T(8,128)}), f32[2,32,256]{2,1,0:T(8,128)}) %reduce-scatter.2.cloned.1.call-update) | async-done | bytes 65552 | tf_op jit(solution)/shard_map/reduce_scatter | solution.py:145
  706.0 0.8 multiply_bitcast_fusion
  706.9 0.3 add_reduce_fusion.6
  707.3 2.4 collective-permute-start
  709.7 1.3 collective-permute-start.1
  711.0 3.7 collective-permute-done.1
  714.9 15.2 %collective-permute-start.2 = (f32[3,4,1]{2,1,0:T(4,128)S(1)}, f32[3,4,1]{2,1,0:T(4,128)S(1)}, u32[]{:S(2)}, u32[]{:S(2)}) collective-permute-start(f32[3,4,1]{2,1,0:T(4,128)S(1)} %get-tuple-element.34), channel_id=1, source_target_pairs={{0,1},{1,2},{2,3},{3,4},{4,5},{5,6},{6,7},{8,9},{9,10},{10,11},{11... | collective-permute-start | bytes 152 | tf_op jit(solution)/shard_map/ppermute | solution.py:20
  730.0 1.9 collective-permute-start.3
  731.9 0.1 maximum_maximum_fusion
  732.0 2.9 collective-permute-done.3
  735.0 0.1 fusion.38
  735.2 3.6 collective-permute-start.4
  738.8 1.3 collective-permute-start.5
  740.1 3.0 collective-permute-done.5
  743.2 3.4 collective-permute-start.6
  746.6 1.9 collective-permute-start.7
  748.6 0.1 maximum_maximum_fusion.1
  748.7 2.9 collective-permute-done.7
  751.6 0.1 fusion.40
  751.8 4.1 collective-permute-start.8
  755.8 1.3 collective-permute-start.9
  757.2 3.3 collective-permute-done.9
  760.6 3.1 collective-permute-start.10
  763.7 1.9 collective-permute-start.11
  765.6 0.1 maximum_maximum_fusion.2
  765.7 2.9 collective-permute-done.11
  768.6 0.1 fusion.42
  768.7 0.7 fusion.50
  (33 shorter events, 0.6 us)
Async XLA Ops:
  6.5 1.6 copy-start
  6.5 699.5 %reduce-scatter.2.cloned.1.call-start = ((), (), s32[]{:S(2)}) async-start(), calls=%async_computation.1 | async-start | bytes 4259840 | tf_op jit(solution)/shard_map/reduce_scatter | solution.py:145
  11.4 0.7 copy-start.3
  11.4 0.7 copy-start.1
  11.5 0.7 copy-start.2
  707.3 3.7 collective-permute-start
  709.7 5.1 collective-permute-start.1
  714.9 17.1 %collective-permute-start.2 = (f32[3,4,1]{2,1,0:T(4,128)S(1)}, f32[3,4,1]{2,1,0:T(4,128)S(1)}, u32[]{:S(2)}, u32[]{:S(2)}) collective-permute-start(f32[3,4,1]{2,1,0:T(4,128)S(1)} %get-tuple-element.34), channel_id=1, source_target_pairs={{0,1},{1,2},{2,3},{3,4},{4,5},{5,6},{6,7},{8,9},{9,10},{10,11},{11... | collective-permute-start | bytes 152 | tf_op jit(solution)/shard_map/ppermute | solution.py:20
  730.0 4.9 collective-permute-start.3
  735.2 4.9 collective-permute-start.4
  738.8 4.3 collective-permute-start.5
  743.2 5.3 collective-permute-start.6
  746.6 4.9 collective-permute-start.7
  751.8 5.4 collective-permute-start.8
  755.8 4.6 collective-permute-start.9
  760.6 5.0 collective-permute-start.10
  763.7 4.9 collective-permute-start.11
Sparse Core Ops, SparseCore 0:
  11.8 694.2 reduce-scatter.1
where the time goes:
time: 777 us; the launch traced here: 776 us
  waiting for transfers between devices  713 us (92%)
  starting transfers between devices  41.3 us (5%)
  between operations  13.7 us (2%)
    reduce_scatter x1, waiting for transfers between devices, on_device(): lax.psum_scatter(jnp.einsum('kt,trc->rkc', table_here, frames, preferred_...  694 us
    ppermute x6, starting transfers between devices, with_halo(): lax.ppermute(lax.slice_in_dim(block, block.shape[dim] - width, None, axis...  31.7 us
    ppermute x6, waiting for transfers between devices, with_halo(): lax.ppermute(lax.slice_in_dim(block, 0, width, axis=dim), axis, backward)  18.8 us
  transfers between devices with their start and end apart: 13, of which 7 were waited for; matrix products, arithmetic and copies ran while one was open for 0% of the time, Pallas kernels for 0%

commit v1 on v0

v1 whole, which is shorter than its diff:
```python
import math

import jax
import jax.numpy as jnp
import numpy as np
from jax import lax
from jax.experimental import pallas as pl
from jax.experimental.pallas import tpu as pltpu
from jax.sharding import Mesh, PartitionSpec as P

TV_PASSES = 3
EPS_TV = 1.0
STEP_TV = 0.2
CLASSES = 4
TM = ("x", "z")


def angle_table(freqs, times, total):
    phase = freqs[:, None] * times[None, :] % total
    angle = phase.astype(jnp.float32) * (2.0 * math.pi / total)
    return jnp.concatenate([jnp.cos(angle), -jnp.sin(angle)], axis=0).astype(jnp.bfloat16)


def start_params(classes):
    level = classes.astype(jnp.float32)
    return jnp.stack([-0.3 + 0.2 * level, 0.5 - 0.3 * level, -0.5 + 0.25 * level])


def model_pieces(start, freqs):
    alpha_par, beta_par, gamma_par = (start[0], start[1], start[2])
    weight = jnp.sqrt(freqs.astype(jnp.float32) / 8.0)[:, None]
    amp = jnp.exp(alpha_par)
    tanh_b = jnp.tanh(beta_par)
    refl = 0.8 * tanh_b
    slope = 0.8 * (1.0 - tanh_b * tanh_b)
    depth = jnp.exp(gamma_par) * weight
    decay = jnp.exp(-2.0 * depth)
    e_re = decay * jnp.cos(2.0 * depth)
    e_im = -decay * jnp.sin(2.0 * depth)
    g_re = refl * e_re
    g_im = refl * e_im
    d_re = 1.0 - g_re
    d_im = -g_im
    denom = d_re * d_re + d_im * d_im
    q_re = ((1.0 + g_re) * d_re + g_im * d_im) / denom
    q_im = (g_im * d_re - (1.0 + g_re) * d_im) / denom
    scale = amp / (math.sqrt(2.0) * weight)

    def project(z_re, z_im):
        return jnp.concatenate([scale * (z_re + z_im), scale * (z_im - z_re)], axis=0)

    den_sq = denom * denom
    p_re = 2.0 * (d_re * d_re - d_im * d_im) / den_sq
    p_im = -4.0 * d_re * d_im / den_sq
    zb_re = (p_re * e_re - p_im * e_im) * slope
    zb_im = (p_re * e_im + p_im * e_re) * slope
    h_re = -2.0 * depth * (g_re - g_im)
    h_im = -2.0 * depth * (g_re + g_im)
    zc_re = p_re * h_re - p_im * h_im
    zc_im = p_re * h_im + p_im * h_re
    return jnp.stack([project(q_re, q_im), project(zb_re, zb_im), project(zc_re, zc_im)])


def class_system(freqs, total_frames):
    start = start_params(jnp.arange(CLASSES, dtype=jnp.int32))
    jac = model_pieces(start, freqs)
    mat = jnp.sum(jac[:, None] * jac[None, :], axis=2)
    damping = 0.1 * (mat[0, 0] + mat[1, 1] + mat[2, 2]) / 3.0 + 0.01
    a00 = mat[0, 0] + damping
    a11 = mat[1, 1] + damping
    a22 = mat[2, 2] + damping
    a01 = mat[0, 1]
    a02 = mat[0, 2]
    a12 = mat[1, 2]
    c00 = a11 * a22 - a12 * a12
    c01 = a02 * a12 - a01 * a22
    c02 = a01 * a12 - a02 * a11
    c11 = a00 * a22 - a02 * a02
    c12 = a01 * a02 - a00 * a12
    c22 = a00 * a11 - a01 * a01
    determinant = a00 * c00 + a01 * c01 + a02 * c02
    inverse = jnp.stack(
        [jnp.stack([c00, c01, c02]), jnp.stack([c01, c11, c12]), jnp.stack([c02, c12, c22])]
    ) / determinant
    model_rhs = mat[:, 0]
    offset = jnp.sum(inverse * model_rhs[None], axis=1)
    rows = jnp.sum(inverse[:, :, None, :] * jac[None], axis=1) / math.sqrt(total_frames)
    return start, offset, rows


def split_terms(value):
    terms = []
    for _ in range(3):
        term = lax.reduce_precision(value, 8, 7)
        terms.append(term.astype(jnp.bfloat16))
        value = value - term
    return jnp.concatenate(terms, axis=0)


def project_kernel(place_ref, weights_ref, frames_ref, *outs):
    group = 16
    count, _, cols = frames_ref.shape
    sums = weights_ref.shape[0]
    tall, wide = sums * group, count * group
    pick_row = lax.broadcasted_iota(jnp.int32, (tall, sums), 0) // group
    pick_col = lax.broadcasted_iota(jnp.int32, (tall, sums), 1)
    spread_rows = (pick_row == pick_col).astype(jnp.float32).astype(jnp.bfloat16)
    copy_row = lax.broadcasted_iota(jnp.int32, (count, wide), 0)
    copy_col = lax.broadcasted_iota(jnp.int32, (count, wide), 1) // group
    spread_cols = (copy_row == copy_col).astype(jnp.float32).astype(jnp.bfloat16)
    tall_by = jnp.dot(spread_rows, weights_ref[...], preferred_element_type=jnp.float32)
    full = jnp.dot(tall_by.astype(jnp.bfloat16), spread_cols, preferred_element_type=jnp.float32)
    same = (
        lax.broadcasted_iota(jnp.int32, (tall, wide), 0) % group
        == lax.broadcasted_iota(jnp.int32, (tall, wide), 1) % group
    )
    matrix = jnp.where(same, full, 0.0).astype(jnp.bfloat16)
    third = tall // 3
    parts = len(outs)
    for shift, out_ref in enumerate(outs):
        rows = out_ref.shape[1]
        first = lax.rem(place_ref[0] + shift, parts) * rows
        for step in range(rows // group):
            begin = pl.multiple_of(first + step * group, group)
            block = frames_ref[:, pl.ds(begin, group), :].reshape(wide, cols)
            got = jnp.dot(matrix, block, preferred_element_type=jnp.float32)
            total = (got[2 * third :] + got[third : 2 * third]) + got[:third]
            out_ref[:, step * group : (step + 1) * group, :] = total.reshape(sums // 3, group, cols)


def project(place, weights, frames, parts):
    count, rows, cols = frames.shape
    sums = weights.shape[0] // 3
    vmem = pl.BlockSpec(memory_space=pltpu.VMEM)
    out = jax.ShapeDtypeStruct((sums, rows // parts, cols), jnp.float32)
    return pl.pallas_call(
        project_kernel,
        out_shape=[out] * parts,
        in_specs=[pl.BlockSpec(memory_space=pltpu.SMEM), vmem, vmem],
        out_specs=[vmem] * parts,
        compiler_params=pltpu.CompilerParams(vmem_limit_bytes=32 * 1024 * 1024),
        cost_estimate=pl.CostEstimate(
            flops=2 * 16 * weights.shape[0] * count * rows * cols,
            bytes_accessed=2 * frames.size + 4 * sums * rows * cols,
            transcendentals=0,
        ),
    )(place, weights, frames)


def shifted(block, axis, count, by):
    pairs = [(i, i + by) for i in range(count) if 0 <= i + by < count]
    return lax.ppermute(block, axis, pairs)


def tv_pass(field, fitted, row_first, col_first, rows_all, cols_all):
    rows = field.shape[1] - 1
    cols = field.shape[2] - 1
    here = field[:, :rows, :cols]
    row_ids = row_first + lax.broadcasted_iota(jnp.int32, (1, rows, cols), 1)
    col_ids = col_first + lax.broadcasted_iota(jnp.int32, (1, rows, cols), 2)
    grad_x = field[:, 1:, :cols] - here
    grad_y = field[:, :rows, 1:] - here
    grad_x = jnp.where((row_ids >= 0) & (row_ids <= rows_all - 2), grad_x, 0.0)
    grad_y = jnp.where((col_ids >= 0) & (col_ids <= cols_all - 2), grad_y, 0.0)
    length = jnp.sqrt(grad_x * grad_x + grad_y * grad_y + EPS_TV * EPS_TV)
    flux_x = grad_x / length
    flux_y = grad_y / length
    diverge = flux_x[:, 1:, 1:] - flux_x[:, :-1, 1:] + flux_y[:, 1:, 1:] - flux_y[:, 1:, :-1]
    inner = field[:, 1:rows, 1:cols]
    return inner + STEP_TV * (diverge - (inner - fitted))


def on_device(frames, freqs, valid, classes):
    frame_count = frames.shape[0]
    x_devs = lax.axis_size("x")
    z_devs = lax.axis_size("z")
    time_devs = x_devs * z_devs
    strip_devs = lax.axis_size("strip")
    total_frames = frame_count * time_devs
    tile_rows, tile_cols = valid.shape
    x_here = lax.axis_index("x")
    tm_here = lax.axis_index(TM)

    classes_z = lax.all_to_all(
        jnp.broadcast_to(classes[None], (z_devs, tile_rows, tile_cols)), "z", 0, 0, tiled=True
    )

    start, offset, rows = class_system(freqs, total_frames)
    times_here = tm_here * frame_count + jnp.arange(frame_count, dtype=jnp.int32)
    table_here = angle_table(freqs, times_here, total_frames).astype(jnp.float32)
    by_class = jnp.transpose(rows, (2, 0, 1)).reshape(CLASSES * 3, -1)
    weights = jnp.sum(by_class[:, :, None] * table_here[None], axis=1)
    place = jnp.full((1,), x_here, jnp.int32)
    sums = project(place, split_terms(weights), frames, x_devs)

    total = sums[0]
    for shift in range(1, x_devs):
        pairs = [(i, (i + shift) % x_devs) for i in range(x_devs)]
        total = total + lax.ppermute(sums[shift], "x", pairs)
    total = total.reshape(CLASSES, 3, z_devs, tile_rows, tile_cols)
    own = jnp.zeros(total.shape[1:], jnp.float32)
    for level in range(CLASSES):
        own = jnp.where((classes_z == level)[None], total[level], own)
    own = jnp.transpose(own, (1, 0, 2, 3))
    own = lax.all_to_all(own, "z", 0, 0, tiled=True)
    delta = jnp.sum(own, axis=0)
    here = start_params(classes)
    base = jnp.zeros_like(here)
    for level in range(CLASSES):
        base = jnp.where((classes == level)[None], offset[:, level][:, None, None], base)
    fitted = jnp.where(valid[None] == 1, here + (delta - base), here)

    wide = TV_PASSES
    left = shifted(fitted[:, :, tile_cols - wide :], "strip", strip_devs, 1)
    right = shifted(fitted[:, :, :wide], "strip", strip_devs, -1)
    band = jnp.concatenate([left, fitted, right], axis=2)
    pieces = [
        shifted(band[:, 1:], TM, time_devs, 2),
        shifted(band, TM, time_devs, 1),
        band,
        shifted(band, TM, time_devs, -1),
        shifted(band[:, :1], TM, time_devs, -2),
    ]
    field = jnp.concatenate(pieces, axis=1)
    row_first = tm_here * tile_rows - wide
    col_first = lax.axis_index("strip") * tile_cols - wide
    rows_all = tile_rows * time_devs
    cols_all = tile_cols * strip_devs
    fit = field
    for step in range(TV_PASSES):
        fit = fit[:, 1:-1, 1:-1]
        field = tv_pass(field, fit, row_first + step, col_first + step, rows_all, cols_all)
    return field


def solution(mesh):
    strip_devs = mesh.shape["strip"]
    x_devs = 4
    grid = Mesh(mesh.devices.reshape(x_devs, -1, strip_devs), ("x", "z", "strip"))
    placed = (P(TM, None, "strip"), P(), P(TM, "strip"), P(TM, "strip"))
    return jax.shard_map(
        on_device, mesh=grid, in_specs=placed, out_specs=P(None, TM, "strip"), check_vma=False
    )
```

time: 777 us -> 89.6 us (0.12)
  waiting for transfers between devices: 713 us -> 29.6 us
  between operations: 13.7 us -> 0.48 us
    reduce_scatter x1 -> x0, waiting for transfers between devices: 694 us -> none  [on_device(): lax.psum_scatter(jnp.einsum('kt,trc->rkc', table_here, frames, preferred_...]
    all_to_all x0 -> x2, waiting for transfers between devices: none -> 22.8 us  [the longest x1 11.5 us: on_device(): own = lax.all_to_all(own, 'z', 0, 0, tiled=True)]
    all_to_all x0 -> x2, starting transfers between devices: none -> 18.4 us  [the longest x1 14.9 us: on_device(): lax.all_to_all(jnp.broadcast_to(classes[None], (z_devs, tile_rows, tile_c...]
    ppermute x12 -> x9, waiting for transfers between devices: 18.8 us -> 6.74 us  [the longest x6 6.73 us: shifted(): return lax.ppermute(block, axis, pairs)]
    ppermute x12 -> x9, starting transfers between devices: 41.3 us -> 30 us  [the longest x6 18.6 us: shifted(): return lax.ppermute(block, axis, pairs)]
  transfers between devices with their start and end apart: 13 -> 11, of which waited for: 7 -> 4; matrix products, arithmetic and copies ran while one was open for 0% -> 1% of each run, Pallas kernels for 0% -> 0%
where the time goes in v1:
time: 89.6 us; the launch traced here: 87.8 us
  starting transfers between devices  48.4 us (54%)
  waiting for transfers between devices  29.6 us (33%)
  other arithmetic  4.93 us (6%)
  local copies, waits for them, and re-layouts  2.77 us (3%)
  Pallas kernels  1.63 us (2%)
    ppermute x6, starting transfers between devices, shifted(): return lax.ppermute(block, axis, pairs)  18.6 us
    all_to_all x1, starting transfers between devices, on_device(): lax.all_to_all(jnp.broadcast_to(classes[None], (z_devs, tile_rows, tile_c...  14.9 us
    all_to_all x1, waiting for transfers between devices, on_device(): own = lax.all_to_all(own, 'z', 0, 0, tiled=True)  11.5 us
    ppermute x3, starting transfers between devices, on_device(): total = total + lax.ppermute(sums[shift], 'x', pairs)  11.4 us
    all_to_all x1, waiting for transfers between devices, on_device(): lax.all_to_all(jnp.broadcast_to(classes[None], (z_devs, tile_rows, tile_c...  11.3 us
    ppermute x6, waiting for transfers between devices, shifted(): return lax.ppermute(block, axis, pairs)  6.73 us
    all_to_all x1, starting transfers between devices, on_device(): own = lax.all_to_all(own, 'z', 0, 0, tiled=True)  3.51 us
  transfers between devices with their start and end apart: 11, of which 4 were waited for; matrix products, arithmetic and copies ran while one was open for 1% of the time, Pallas kernels for 0%

profile of v1, /device:TPU:1, one launch (start us, length us, event | category | flops | bytes accessed | tf_op | source)
XLA Modules:
  0.0 87.8 jit_solution(17196441331154661019)
XLA Ops:
  0.0 0.7 multiply_sqrt_fusion
  0.7 0.1 add_multiply_fusion.3
  1.0 0.1 multiply_reduce_fusion.2
  1.4 0.8 cosine_convert_fusion
  2.2 0.1 multiply_reduce_fusion
  2.4 1.6 %copy-done = bf16[32,128,256]{2,1,0:T(8,128)(2,1)S(1)} copy-done((bf16[32,128,256]{2,1,0:T(8,128)(2,1)S(1)}, bf16[32,128,256]{2,1,0:T(8,128)(2,1)}, u32[]{:S(2)}) %copy-start) | copy-done | bytes 2097176
  3.9 1.6 %shard_map.46 = (f32[12,32,256]{2,1,0:T(8,128)S(1)}, f32[12,32,256]{2,1,0:T(8,128)S(1)}, f32[12,32,256]{2,1,0:T(8,128)S(1)}, f32[12,32,256]{2,1,0:T(8,128)S(1)}) custom-call(s32[1]{0:T(128)} %bitcast.3.place_ref, bf16[36,32]{1,0:T(8,128)(2,1)S(1)} %pad_maximum_fusion.7.weights_ref, bf16[32,128,256]{2,1,0:T(8,128)(2,1)S(1)} %copy-done), custom_call_target="tpu_custom_call" | custom-call | flops 1207959552 | bytes 3670016 | tf_op jit(solution)/shard_map/pallas_call | solution.py:136
  5.6 3.9 %collective-permute-start = (f32[12,32,256]{2,1,0:T(8,128)S(1)}, f32[12,32,256]{2,1,0:T(8,128)S(1)}, u32[]{:S(2)}, u32[]{:S(2)}) collective-permute-start(f32[12,32,256]{2,1,0:T(8,128)S(1)} %get-tuple-element.10), channel_id=1, source_target_pairs={{0,128},{128,256},{256,384},{384,0},{1,129},{129,257},{257,385},{3... | collective-permute-start | bytes 1179656 | tf_op jit(solution)/shard_map/ppermute | solution.py:199
  9.5 4.4 %collective-permute-start.1 = (f32[12,32,256]{2,1,0:T(8,128)S(1)}, f32[12,32,256]{2,1,0:T(8,128)S(1)}, u32[]{:S(2)}, u32[]{:S(2)}) collective-permute-start(f32[12,32,256]{2,1,0:T(8,128)S(1)} %get-tuple-element.11), channel_id=1, source_target_pairs={{0,256},{128,384},{256,0},{384,128},{1,257},{129,385},{257,1},{385... | collective-permute-start | bytes 1179656 | tf_op jit(solution)/shard_map/ppermute | solution.py:199
  13.9 3.1 %collective-permute-start.2 = (f32[12,32,256]{2,1,0:T(8,128)S(1)}, f32[12,32,256]{2,1,0:T(8,128)S(1)}, u32[]{:S(2)}, u32[]{:S(2)}) collective-permute-start(f32[12,32,256]{2,1,0:T(8,128)S(1)} %get-tuple-element.12), channel_id=1, source_target_pairs={{0,384},{128,0},{256,128},{384,256},{1,385},{129,1},{257,129},{385... | collective-permute-start | bytes 1179656 | tf_op jit(solution)/shard_map/ppermute | solution.py:199
  17.0 0.6 broadcast_in_dim.179
  17.6 14.9 %all-to-all-start = ((s32[16,2,256]{2,1,0:T(2,128)}), s32[16,2,256]{2,1,0:T(2,128)S(1)}, u32[]{:S(2)}, u32[]{:S(2)}) async-start(s32[16,2,256]{2,1,0:T(2,128)} %broadcast_in_dim.179), calls=%async_computation | async-start | bytes 65536 | tf_op jit(solution)/shard_map/all_to_all | solution.py:184
  32.7 11.3 %all-to-all-done = s32[16,2,256]{2,1,0:T(2,128)S(1)} async-done(((s32[16,2,256]{2,1,0:T(2,128)}), s32[16,2,256]{2,1,0:T(2,128)S(1)}, u32[]{:S(2)}, u32[]{:S(2)}) %all-to-all-start) | async-done | bytes 32800 | tf_op jit(solution)/shard_map/all_to_all | solution.py:184
  44.1 0.1 add_add_fusion
  44.5 0.8 fusion
  45.3 3.5 %all-to-all-start.1 = ((f32[16,3,2,256]{3,2,1,0:T(2,128)}), f32[16,3,2,256]{3,2,1,0:T(2,128)S(1)}, u32[]{:S(2)}, u32[]{:S(2)}) async-start(f32[16,3,2,256]{3,2,1,0:T(2,128)} %fusion), calls=%async_computation.1 | async-start | bytes 196608 | tf_op jit(solution)/shard_map/all_to_all | solution.py:205
  48.9 0.2 slice_reduce_fusion
  49.1 11.5 %all-to-all-done.1 = f32[16,3,2,256]{3,2,1,0:T(2,128)S(1)} async-done(((f32[16,3,2,256]{3,2,1,0:T(2,128)}), f32[16,3,2,256]{3,2,1,0:T(2,128)S(1)}, u32[]{:S(2)}, u32[]{:S(2)}) %all-to-all-start.1) | async-done | bytes 98336 | tf_op jit(solution)/shard_map/all_to_all | solution.py:205
  60.8 7.2 %collective-permute-start.3 = (f32[3,2,3]{2,1,0:T(2,128)S(1)}, f32[3,2,3]{2,1,0:T(2,128)S(1)}, u32[]{:S(2)}, u32[]{:S(2)}) collective-permute-start(f32[3,2,3]{2,1,0:T(2,128)S(1)} %get-tuple-element.45), channel_id=1, source_target_pairs={{0,1},{1,2},{2,3},{3,4},{4,5},{5,6},{6,7},{8,9},{9,10},{10,11},{11... | collective-permute-start | bytes 224 | tf_op jit(solution)/shard_map/ppermute | solution.py:152
  68.0 1.9 %collective-permute-start.4 = (f32[3,2,3]{2,1,0:T(2,128)S(1)}, f32[3,2,3]{2,1,0:T(2,128)S(1)}, u32[]{:S(2)}, u32[]{:S(2)}) collective-permute-start(f32[3,2,3]{2,1,0:T(2,128)S(1)} %get-tuple-element.46), channel_id=1, source_target_pairs={{1,0},{2,1},{3,2},{4,3},{5,4},{6,5},{7,6},{9,8},{10,9},{11,10},{12... | collective-permute-start | bytes 224 | tf_op jit(solution)/shard_map/ppermute | solution.py:152
  70.0 3.0 %collective-permute-done.4 = f32[3,2,3]{2,1,0:T(2,128)S(1)} collective-permute-done((f32[3,2,3]{2,1,0:T(2,128)S(1)}, f32[3,2,3]{2,1,0:T(2,128)S(1)}, u32[]{:S(2)}, u32[]{:S(2)}) %collective-permute-start.4) | collective-permute-done | bytes 104 | tf_op jit(solution)/shard_map/ppermute | solution.py:152
  73.0 2.7 %collective-permute-start.5 = (f32[3,2,262]{2,1,0:T(2,128)S(1)}, f32[3,2,262]{2,1,0:T(2,128)S(1)}, u32[]{:S(2)}, u32[]{:S(2)}) collective-permute-start(f32[3,2,262]{2,1,0:T(2,128)S(1)} %pad_maximum_fusion.8), channel_id=1, source_target_pairs={{0,8},{8,16},{16,24},{24,32},{32,40},{40,48},{48,56},{56,64},{64,7... | collective-permute-start | bytes 18872 | tf_op jit(solution)/shard_map/ppermute | solution.py:152
  75.8 1.3 %collective-permute-start.6 = (f32[3,2,262]{2,1,0:T(2,128)S(1)}, f32[3,2,262]{2,1,0:T(2,128)S(1)}, u32[]{:S(2)}, u32[]{:S(2)}) collective-permute-start(f32[3,2,262]{2,1,0:T(2,128)S(1)} %pad_maximum_fusion.8), channel_id=1, source_target_pairs={{8,0},{16,8},{24,16},{32,24},{40,32},{48,40},{56,48},{64,56},{72,6... | collective-permute-start | bytes 18872 | tf_op jit(solution)/shard_map/ppermute | solution.py:152
  77.1 4.2 %collective-permute-start.8 = (f32[3,1,262]{2,1,0:T(1,128)S(1)}, f32[3,1,262]{2,1,0:T(1,128)S(1)}, u32[]{:S(2)}, u32[]{:S(2)}) collective-permute-start(f32[3,1,262]{2,1,0:T(1,128)S(1)} %get-tuple-element.36), channel_id=1, source_target_pairs={{0,16},{8,24},{16,32},{24,40},{32,48},{40,56},{48,64},{56,72},{64,... | collective-permute-start | bytes 9440 | tf_op jit(solution)/shard_map/ppermute | solution.py:152
  81.2 1.3 %collective-permute-start.7 = (f32[3,1,262]{2,1,0:T(1,128)S(1)}, f32[3,1,262]{2,1,0:T(1,128)S(1)}, u32[]{:S(2)}, u32[]{:S(2)}) collective-permute-start(f32[3,1,262]{2,1,0:T(1,128)S(1)} %get-tuple-element.35), channel_id=1, source_target_pairs={{16,0},{24,8},{32,16},{40,24},{48,32},{56,40},{64,48},{72,56},{80,... | collective-permute-start | bytes 9440 | tf_op jit(solution)/shard_map/ppermute | solution.py:152
  82.8 3.7 %collective-permute-done.7 = f32[3,1,262]{2,1,0:T(1,128)S(1)} collective-permute-done((f32[3,1,262]{2,1,0:T(1,128)S(1)}, f32[3,1,262]{2,1,0:T(1,128)S(1)}, u32[]{:S(2)}, u32[]{:S(2)}) %collective-permute-start.7) | collective-permute-done | bytes 3176 | tf_op jit(solution)/shard_map/ppermute | solution.py:152
  86.5 0.1 fusion.12
  86.6 0.1 fusion.5
  86.7 0.1 fusion.10
  86.9 0.1 fusion.17
  87.0 0.1 fusion.19
  87.1 0.7 fusion.27
  (56 shorter events, 1.3 us)
Async XLA Ops:
  2.3 1.6 %copy-start = (bf16[32,128,256]{2,1,0:T(8,128)(2,1)S(1)}, bf16[32,128,256]{2,1,0:T(8,128)(2,1)}, u32[]{:S(2)}) copy-start(bf16[32,128,256]{2,1,0:T(8,128)(2,1)} %frames_ref.1) | copy-start | bytes 6291460
  3.9 13.0 %copy-start.1 = (s32[2,256]{1,0:T(2,128)S(1)}, s32[2,256]{1,0:T(2,128)}, u32[]{:S(2)}) copy-start(s32[2,256]{1,0:T(2,128)} %param.7) | copy-start | bytes 6148
  3.9 28.6 %copy-start.2 = (s32[2,256]{1,0:T(2,128)S(1)}, s32[2,256]{1,0:T(2,128)}, u32[]{:S(2)}) copy-start(s32[2,256]{1,0:T(2,128)} %param.6) | copy-start | bytes 6148
  5.6 38.5 %collective-permute-start = (f32[12,32,256]{2,1,0:T(8,128)S(1)}, f32[12,32,256]{2,1,0:T(8,128)S(1)}, u32[]{:S(2)}, u32[]{:S(2)}) collective-permute-start(f32[12,32,256]{2,1,0:T(8,128)S(1)} %get-tuple-element.10), channel_id=1, source_target_pairs={{0,128},{128,256},{256,384},{384,0},{1,129},{129,257},{257,385},{3... | collective-permute-start | bytes 1179656 | tf_op jit(solution)/shard_map/ppermute | solution.py:199
  9.5 34.5 %collective-permute-start.1 = (f32[12,32,256]{2,1,0:T(8,128)S(1)}, f32[12,32,256]{2,1,0:T(8,128)S(1)}, u32[]{:S(2)}, u32[]{:S(2)}) collective-permute-start(f32[12,32,256]{2,1,0:T(8,128)S(1)} %get-tuple-element.11), channel_id=1, source_target_pairs={{0,256},{128,384},{256,0},{384,128},{1,257},{129,385},{257,1},{385... | collective-permute-start | bytes 1179656 | tf_op jit(solution)/shard_map/ppermute | solution.py:199
  13.9 30.2 %collective-permute-start.2 = (f32[12,32,256]{2,1,0:T(8,128)S(1)}, f32[12,32,256]{2,1,0:T(8,128)S(1)}, u32[]{:S(2)}, u32[]{:S(2)}) collective-permute-start(f32[12,32,256]{2,1,0:T(8,128)S(1)} %get-tuple-element.12), channel_id=1, source_target_pairs={{0,384},{128,0},{256,128},{384,256},{1,385},{129,1},{257,129},{385... | collective-permute-start | bytes 1179656 | tf_op jit(solution)/shard_map/ppermute | solution.py:199
  17.6 26.4 %all-to-all-start = ((s32[16,2,256]{2,1,0:T(2,128)}), s32[16,2,256]{2,1,0:T(2,128)S(1)}, u32[]{:S(2)}, u32[]{:S(2)}) async-start(s32[16,2,256]{2,1,0:T(2,128)} %broadcast_in_dim.179), calls=%async_computation | async-start | bytes 65536 | tf_op jit(solution)/shard_map/all_to_all | solution.py:184
  45.3 15.3 %all-to-all-start.1 = ((f32[16,3,2,256]{3,2,1,0:T(2,128)}), f32[16,3,2,256]{3,2,1,0:T(2,128)S(1)}, u32[]{:S(2)}, u32[]{:S(2)}) async-start(f32[16,3,2,256]{3,2,1,0:T(2,128)} %fusion), calls=%async_computation.1 | async-start | bytes 196608 | tf_op jit(solution)/shard_map/all_to_all | solution.py:205
  60.8 9.2 %collective-permute-start.3 = (f32[3,2,3]{2,1,0:T(2,128)S(1)}, f32[3,2,3]{2,1,0:T(2,128)S(1)}, u32[]{:S(2)}, u32[]{:S(2)}) collective-permute-start(f32[3,2,3]{2,1,0:T(2,128)S(1)} %get-tuple-element.45), channel_id=1, source_target_pairs={{0,1},{1,2},{2,3},{3,4},{4,5},{5,6},{6,7},{8,9},{9,10},{10,11},{11... | collective-permute-start | bytes 224 | tf_op jit(solution)/shard_map/ppermute | solution.py:152
  68.0 4.9 %collective-permute-start.4 = (f32[3,2,3]{2,1,0:T(2,128)S(1)}, f32[3,2,3]{2,1,0:T(2,128)S(1)}, u32[]{:S(2)}, u32[]{:S(2)}) collective-permute-start(f32[3,2,3]{2,1,0:T(2,128)S(1)} %get-tuple-element.46), channel_id=1, source_target_pairs={{1,0},{2,1},{3,2},{4,3},{5,4},{6,5},{7,6},{9,8},{10,9},{11,10},{12... | collective-permute-start | bytes 224 | tf_op jit(solution)/shard_map/ppermute | solution.py:152
  73.0 9.5 %collective-permute-start.5 = (f32[3,2,262]{2,1,0:T(2,128)S(1)}, f32[3,2,262]{2,1,0:T(2,128)S(1)}, u32[]{:S(2)}, u32[]{:S(2)}) collective-permute-start(f32[3,2,262]{2,1,0:T(2,128)S(1)} %pad_maximum_fusion.8), channel_id=1, source_target_pairs={{0,8},{8,16},{16,24},{24,32},{32,40},{40,48},{48,56},{56,64},{64,7... | collective-permute-start | bytes 18872 | tf_op jit(solution)/shard_map/ppermute | solution.py:152
  75.8 6.8 %collective-permute-start.6 = (f32[3,2,262]{2,1,0:T(2,128)S(1)}, f32[3,2,262]{2,1,0:T(2,128)S(1)}, u32[]{:S(2)}, u32[]{:S(2)}) collective-permute-start(f32[3,2,262]{2,1,0:T(2,128)S(1)} %pad_maximum_fusion.8), channel_id=1, source_target_pairs={{8,0},{16,8},{24,16},{32,24},{40,32},{48,40},{56,48},{64,56},{72,6... | collective-permute-start | bytes 18872 | tf_op jit(solution)/shard_map/ppermute | solution.py:152
  77.1 5.6 %collective-permute-start.8 = (f32[3,1,262]{2,1,0:T(1,128)S(1)}, f32[3,1,262]{2,1,0:T(1,128)S(1)}, u32[]{:S(2)}, u32[]{:S(2)}) collective-permute-start(f32[3,1,262]{2,1,0:T(1,128)S(1)} %get-tuple-element.36), channel_id=1, source_target_pairs={{0,16},{8,24},{16,32},{24,40},{32,48},{40,56},{48,64},{56,72},{64,... | collective-permute-start | bytes 9440 | tf_op jit(solution)/shard_map/ppermute | solution.py:152
  81.2 5.3 %collective-permute-start.7 = (f32[3,1,262]{2,1,0:T(1,128)S(1)}, f32[3,1,262]{2,1,0:T(1,128)S(1)}, u32[]{:S(2)}, u32[]{:S(2)}) collective-permute-start(f32[3,1,262]{2,1,0:T(1,128)S(1)} %get-tuple-element.35), channel_id=1, source_target_pairs={{16,0},{24,8},{32,16},{40,24},{48,32},{56,40},{64,48},{72,56},{80,... | collective-permute-start | bytes 9440 | tf_op jit(solution)/shard_map/ppermute | solution.py:152

commit v2 on v1

--- a/solution.py
+++ b/solution.py
@@ -147,6 +147,14 @@
     )(place, weights, frames)
 
 
+def exchange(block, count):
+    middle = count // 2
+    order = [(middle + i) % count for i in range(count)]
+    block = jnp.concatenate([block[middle:], block[:middle]])
+    got = lax.all_to_all(block, "z", 0, 0, axis_index_groups=[order], tiled=True)
+    return jnp.concatenate([got[count - middle :], got[: count - middle]])
+
+
 def shifted(block, axis, count, by):
     pairs = [(i, i + by) for i in range(count) if 0 <= i + by < count]
     return lax.ppermute(block, axis, pairs)
@@ -181,9 +189,8 @@
     x_here = lax.axis_index("x")
     tm_here = lax.axis_index(TM)
 
-    classes_z = lax.all_to_all(
-        jnp.broadcast_to(classes[None], (z_devs, tile_rows, tile_cols)), "z", 0, 0, tiled=True
-    )
+    codes = classes + CLASSES * valid
+    classes_z = exchange(jnp.broadcast_to(codes[None], (z_devs, *codes.shape)), z_devs)
 
     start, offset, rows = class_system(freqs, total_frames)
     times_here = tm_here * frame_count + jnp.arange(frame_count, dtype=jnp.int32)
@@ -197,32 +204,36 @@
     for shift in range(1, x_devs):
         pairs = [(i, (i + shift) % x_devs) for i in range(x_devs)]
         total = total + lax.ppermute(sums[shift], "x", pairs)
-    total = total.reshape(CLASSES, 3, z_devs, tile_rows, tile_cols)
+    pair = 2 * tile_rows
+    total = total.reshape(CLASSES, 3, z_devs // 2, pair, tile_cols)
+    levels = classes_z.reshape(z_devs // 2, pair, tile_cols) % CLASSES
     own = jnp.zeros(total.shape[1:], jnp.float32)
     for level in range(CLASSES):
-        own = jnp.where((classes_z == level)[None], total[level], own)
+        own = jnp.where((levels == level)[None], total[level], own)
     own = jnp.transpose(own, (1, 0, 2, 3))
-    own = lax.all_to_all(own, "z", 0, 0, tiled=True)
+    own = jnp.broadcast_to(own[:, None], (z_devs // 2, 2, *own.shape[1:]))
+    own = own.reshape(z_devs, 3, pair, tile_cols)
+    own = exchange(own, z_devs)
     delta = jnp.sum(own, axis=0)
+    codes = lax.dynamic_index_in_dim(
+        classes_z.reshape(z_devs // 2, pair, tile_cols), lax.axis_index("z") // 2, 0, False
+    )
+    classes = codes % CLASSES
     here = start_params(classes)
     base = jnp.zeros_like(here)
     for level in range(CLASSES):
         base = jnp.where((classes == level)[None], offset[:, level][:, None, None], base)
-    fitted = jnp.where(valid[None] == 1, here + (delta - base), here)
+    fitted = jnp.where((codes >= CLASSES)[None], here + (delta - base), here)
 
     wide = TV_PASSES
     left = shifted(fitted[:, :, tile_cols - wide :], "strip", strip_devs, 1)
     right = shifted(fitted[:, :, :wide], "strip", strip_devs, -1)
     band = jnp.concatenate([left, fitted, right], axis=2)
-    pieces = [
-        shifted(band[:, 1:], TM, time_devs, 2),
-        shifted(band, TM, time_devs, 1),
-        band,
-        shifted(band, TM, time_devs, -1),
-        shifted(band[:, :1], TM, time_devs, -2),
-    ]
-    field = jnp.concatenate(pieces, axis=1)
-    row_first = tm_here * tile_rows - wide
+    above = shifted(band[:, pair - wide :], TM, time_devs, 2)
+    below = shifted(band[:, :wide], TM, time_devs, -2)
+    field = jnp.concatenate([above, band, below], axis=1)
+    pair_first = lax.div(tm_here, 2) * pair
+    row_first = pair_first - wide
     col_first = lax.axis_index("strip") * tile_cols - wide
     rows_all = tile_rows * time_devs
     cols_all = tile_cols * strip_devs
@@ -230,7 +241,7 @@
     for step in range(TV_PASSES):
         fit = fit[:, 1:-1, 1:-1]
         field = tv_pass(field, fit, row_first + step, col_first + step, rows_all, cols_all)
-    return field
+    return lax.dynamic_slice_in_dim(field, tm_here * tile_rows - pair_first, tile_rows, 1)
 
 
 def solution(mesh):

time: 89.6 us -> 82.9 us (0.925); the launches traced: 87.8 us -> 82.5 us
  waiting for transfers between devices: 29.6 us -> 17.2 us
  starting transfers between devices: 48.4 us -> 55.4 us
    all_to_all x2, waiting for transfers between devices: 22.8 us -> 9.65 us  [exchange(): lax.all_to_all(block, 'z', 0, 0, axis_index_groups=[order], tiled=True)]
    all_to_all x2, starting transfers between devices: 18.4 us -> 30.8 us  [exchange(): lax.all_to_all(block, 'z', 0, 0, axis_index_groups=[order], tiled=True)]
    ppermute x6 -> x4, starting transfers between devices: 18.6 us -> 13.2 us  [shifted(): return lax.ppermute(block, axis, pairs)]
    concatenate x2 -> x4, other arithmetic: 0.18 us -> 1.43 us  [the longest x2 1.33 us: exchange(): block = jnp.concatenate([block[middle:], block[:middle]])]
    ppermute x6 -> x4, waiting for transfers between devices: 6.73 us -> 7.53 us  [shifted(): return lax.ppermute(block, axis, pairs)]
  transfers between devices with their start and end apart: 11 -> 9, of which waited for: 4 -> 4; matrix products, arithmetic and copies ran while one was open for 1% -> 1% of each run, Pallas kernels for 0% -> 0%
where the time goes in v2:
time: 82.9 us; the launch traced here: 82.5 us
  starting transfers between devices  55.4 us (67%)
  waiting for transfers between devices  17.2 us (21%)
  other arithmetic  5.35 us (6%)
  local copies, waits for them, and re-layouts  2.38 us (3%)
  Pallas kernels  1.63 us (2%)
    all_to_all x2, starting transfers between devices, exchange(): lax.all_to_all(block, 'z', 0, 0, axis_index_groups=[order], tiled=True)  30.8 us
    ppermute x4, starting transfers between devices, shifted(): return lax.ppermute(block, axis, pairs)  13.2 us
    ppermute x3, starting transfers between devices, on_device(): total = total + lax.ppermute(sums[shift], 'x', pairs)  11.4 us
    all_to_all x2, waiting for transfers between devices, exchange(): lax.all_to_all(block, 'z', 0, 0, axis_index_groups=[order], tiled=True)  9.65 us
    ppermute x4, waiting for transfers between devices, shifted(): return lax.ppermute(block, axis, pairs)  7.53 us
  transfers between devices with their start and end apart: 9, of which 4 were waited for; matrix products, arithmetic and copies ran while one was open for 1% of the time, Pallas kernels for 0%

profile of v2, /device:TPU:1, one launch (start us, length us, event | category | flops | bytes accessed | tf_op | source)
XLA Modules:
  0.0 82.5 jit_solution(8177950748205890289)
XLA Ops:
  0.0 0.7 multiply_sqrt_fusion
  0.7 0.1 add_multiply_fusion.3
  1.0 0.1 multiply_reduce_fusion.2
  1.4 0.8 cosine_convert_fusion
  2.2 0.1 multiply_reduce_fusion
  2.4 1.6 %copy-done = bf16[32,128,256]{2,1,0:T(8,128)(2,1)S(1)} copy-done((bf16[32,128,256]{2,1,0:T(8,128)(2,1)S(1)}, bf16[32,128,256]{2,1,0:T(8,128)(2,1)}, u32[]{:S(2)}) %copy-start) | copy-done | bytes 2097176
  3.9 1.6 %shard_map.46 = (f32[12,32,256]{2,1,0:T(8,128)S(1)}, f32[12,32,256]{2,1,0:T(8,128)S(1)}, f32[12,32,256]{2,1,0:T(8,128)S(1)}, f32[12,32,256]{2,1,0:T(8,128)S(1)}) custom-call(s32[1]{0:T(128)} %bitcast.1.place_ref, bf16[36,32]{1,0:T(8,128)(2,1)S(1)} %pad_maximum_fusion.3.weights_ref, bf16[32,128,256]{2,1,0:T(8,128)(2,1)S(1)} %copy-done), custom_call_target="tpu_custom_call" | custom-call | flops 1207959552 | bytes 3670016 | tf_op jit(solution)/shard_map/pallas_call | solution.py:136
  5.6 3.9 %collective-permute-start = (f32[12,32,256]{2,1,0:T(8,128)S(1)}, f32[12,32,256]{2,1,0:T(8,128)S(1)}, u32[]{:S(2)}, u32[]{:S(2)}) collective-permute-start(f32[12,32,256]{2,1,0:T(8,128)S(1)} %get-tuple-element.10), channel_id=1, source_target_pairs={{0,128},{128,256},{256,384},{384,0},{1,129},{129,257},{257,385},{3... | collective-permute-start | bytes 1179656 | tf_op jit(solution)/shard_map/ppermute | solution.py:206
  9.5 4.4 %collective-permute-start.1 = (f32[12,32,256]{2,1,0:T(8,128)S(1)}, f32[12,32,256]{2,1,0:T(8,128)S(1)}, u32[]{:S(2)}, u32[]{:S(2)}) collective-permute-start(f32[12,32,256]{2,1,0:T(8,128)S(1)} %get-tuple-element.11), channel_id=1, source_target_pairs={{0,256},{128,384},{256,0},{384,128},{1,257},{129,385},{257,1},{385... | collective-permute-start | bytes 1179656 | tf_op jit(solution)/shard_map/ppermute | solution.py:206
  13.9 3.1 %collective-permute-start.2 = (f32[12,32,256]{2,1,0:T(8,128)S(1)}, f32[12,32,256]{2,1,0:T(8,128)S(1)}, u32[]{:S(2)}, u32[]{:S(2)}) collective-permute-start(f32[12,32,256]{2,1,0:T(8,128)S(1)} %get-tuple-element.12), channel_id=1, source_target_pairs={{0,384},{128,0},{256,128},{384,256},{1,385},{129,1},{257,129},{385... | collective-permute-start | bytes 1179656 | tf_op jit(solution)/shard_map/ppermute | solution.py:206
  17.0 0.6 pad_add_fusion
  17.6 18.3 %all-to-all-start = ((s32[16,2,256]{2,1,0:T(2,128)}), s32[16,2,256]{2,1,0:T(2,128)S(1)}, u32[]{:S(2)}, u32[]{:S(2)}) async-start(s32[16,2,256]{2,1,0:T(2,128)} %pad_add_fusion), calls=%async_computation | async-start | bytes 65536 | tf_op jit(solution)/shard_map/all_to_all | solution.py:154
  36.0 2.4 %all-to-all-done = s32[16,2,256]{2,1,0:T(2,128)S(1)} async-done(((s32[16,2,256]{2,1,0:T(2,128)}), s32[16,2,256]{2,1,0:T(2,128)S(1)}, u32[]{:S(2)}, u32[]{:S(2)}) %all-to-all-start) | async-done | bytes 32800 | tf_op jit(solution)/shard_map/all_to_all | solution.py:154
  38.5 0.1 add_add_fusion
  39.0 0.7 pad_maximum_fusion
  39.7 12.5 %all-to-all-start.1 = ((f32[16,3,4,256]{3,2,1,0:T(4,128)}), f32[16,3,4,256]{3,2,1,0:T(4,128)S(1)}, u32[]{:S(2)}, u32[]{:S(2)}) async-start(f32[16,3,4,256]{3,2,1,0:T(4,128)} %pad_maximum_fusion), calls=%async_computation.1 | async-start | bytes 393216 | tf_op jit(solution)/shard_map/all_to_all | solution.py:154
  52.2 0.2 slice_reduce_fusion.5
  52.5 7.3 %all-to-all-done.1 = f32[16,3,4,256]{3,2,1,0:T(4,128)S(1)} async-done(((f32[16,3,4,256]{3,2,1,0:T(4,128)}), f32[16,3,4,256]{3,2,1,0:T(4,128)S(1)}, u32[]{:S(2)}, u32[]{:S(2)}) %all-to-all-start.1) | async-done | bytes 196640 | tf_op jit(solution)/shard_map/all_to_all | solution.py:154
  59.8 0.1 add_select_fusion.1
  60.0 6.1 %collective-permute-start.3 = (f32[3,4,3]{2,1,0:T(4,128)S(1)}, f32[3,4,3]{2,1,0:T(4,128)S(1)}, u32[]{:S(2)}, u32[]{:S(2)}) collective-permute-start(f32[3,4,3]{2,1,0:T(4,128)S(1)} %get-tuple-element.51), channel_id=1, source_target_pairs={{0,1},{1,2},{2,3},{3,4},{4,5},{5,6},{6,7},{8,9},{9,10},{10,11},{11... | collective-permute-start | bytes 440 | tf_op jit(solution)/shard_map/ppermute | solution.py:160
  66.1 1.9 %collective-permute-start.4 = (f32[3,4,3]{2,1,0:T(4,128)S(1)}, f32[3,4,3]{2,1,0:T(4,128)S(1)}, u32[]{:S(2)}, u32[]{:S(2)}) collective-permute-start(f32[3,4,3]{2,1,0:T(4,128)S(1)} %get-tuple-element.52), channel_id=1, source_target_pairs={{1,0},{2,1},{3,2},{4,3},{5,4},{6,5},{7,6},{9,8},{10,9},{11,10},{12... | collective-permute-start | bytes 440 | tf_op jit(solution)/shard_map/ppermute | solution.py:160
  68.0 3.0 %collective-permute-done.4 = f32[3,4,3]{2,1,0:T(4,128)S(1)} collective-permute-done((f32[3,4,3]{2,1,0:T(4,128)S(1)}, f32[3,4,3]{2,1,0:T(4,128)S(1)}, u32[]{:S(2)}, u32[]{:S(2)}) %collective-permute-start.4) | collective-permute-done | bytes 176 | tf_op jit(solution)/shard_map/ppermute | solution.py:160
  71.1 4.0 %collective-permute-start.5 = (f32[3,3,262]{2,1,0:T(4,128)S(1)}, f32[3,3,262]{2,1,0:T(4,128)S(1)}, u32[]{:S(2)}, u32[]{:S(2)}) collective-permute-start(f32[3,3,262]{2,1,0:T(4,128)S(1)} %get-tuple-element.49), channel_id=1, source_target_pairs={{0,16},{8,24},{16,32},{24,40},{32,48},{40,56},{48,64},{56,72},{64,... | collective-permute-start | bytes 28304 | tf_op jit(solution)/shard_map/ppermute | solution.py:160
  75.1 1.3 %collective-permute-start.6 = (f32[3,3,262]{2,1,0:T(4,128)S(1)}, f32[3,3,262]{2,1,0:T(4,128)S(1)}, u32[]{:S(2)}, u32[]{:S(2)}) collective-permute-start(f32[3,3,262]{2,1,0:T(4,128)S(1)} %get-tuple-element.50), channel_id=1, source_target_pairs={{16,0},{24,8},{32,16},{40,24},{48,32},{56,40},{64,48},{72,56},{80,... | collective-permute-start | bytes 28304 | tf_op jit(solution)/shard_map/ppermute | solution.py:160
  76.4 4.5 %collective-permute-done.6 = f32[3,3,262]{2,1,0:T(4,128)S(1)} collective-permute-done((f32[3,3,262]{2,1,0:T(4,128)S(1)}, f32[3,3,262]{2,1,0:T(4,128)S(1)}, u32[]{:S(2)}, u32[]{:S(2)}) %collective-permute-start.6) | collective-permute-done | bytes 9464 | tf_op jit(solution)/shard_map/ppermute | solution.py:160
  80.9 0.1 pad_maximum_fusion.1
  81.0 0.1 fusion.3
  81.2 0.1 fusion.13
  81.3 0.1 fusion.17
  81.4 0.1 fusion.8
  81.6 0.1 fusion.15
  81.9 0.6 fusion.26
  (66 shorter events, 1.3 us)
Async XLA Ops:
  2.3 1.6 %copy-start = (bf16[32,128,256]{2,1,0:T(8,128)(2,1)S(1)}, bf16[32,128,256]{2,1,0:T(8,128)(2,1)}, u32[]{:S(2)}) copy-start(bf16[32,128,256]{2,1,0:T(8,128)(2,1)} %frames_ref.1) | copy-start | bytes 6291460
  3.9 13.0 %copy-start.1 = (s32[2,256]{1,0:T(2,128)S(1)}, s32[2,256]{1,0:T(2,128)}, u32[]{:S(2)}) copy-start(s32[2,256]{1,0:T(2,128)} %param.7) | copy-start | bytes 6148
  3.9 13.0 %copy-start.2 = (s32[2,256]{1,0:T(2,128)S(1)}, s32[2,256]{1,0:T(2,128)}, u32[]{:S(2)}) copy-start(s32[2,256]{1,0:T(2,128)} %param.6) | copy-start | bytes 6148
  5.6 32.9 %collective-permute-start = (f32[12,32,256]{2,1,0:T(8,128)S(1)}, f32[12,32,256]{2,1,0:T(8,128)S(1)}, u32[]{:S(2)}, u32[]{:S(2)}) collective-permute-start(f32[12,32,256]{2,1,0:T(8,128)S(1)} %get-tuple-element.10), channel_id=1, source_target_pairs={{0,128},{128,256},{256,384},{384,0},{1,129},{129,257},{257,385},{3... | collective-permute-start | bytes 1179656 | tf_op jit(solution)/shard_map/ppermute | solution.py:206
  9.5 29.0 %collective-permute-start.1 = (f32[12,32,256]{2,1,0:T(8,128)S(1)}, f32[12,32,256]{2,1,0:T(8,128)S(1)}, u32[]{:S(2)}, u32[]{:S(2)}) collective-permute-start(f32[12,32,256]{2,1,0:T(8,128)S(1)} %get-tuple-element.11), channel_id=1, source_target_pairs={{0,256},{128,384},{256,0},{384,128},{1,257},{129,385},{257,1},{385... | collective-permute-start | bytes 1179656 | tf_op jit(solution)/shard_map/ppermute | solution.py:206
  13.9 24.6 %collective-permute-start.2 = (f32[12,32,256]{2,1,0:T(8,128)S(1)}, f32[12,32,256]{2,1,0:T(8,128)S(1)}, u32[]{:S(2)}, u32[]{:S(2)}) collective-permute-start(f32[12,32,256]{2,1,0:T(8,128)S(1)} %get-tuple-element.12), channel_id=1, source_target_pairs={{0,384},{128,0},{256,128},{384,256},{1,385},{129,1},{257,129},{385... | collective-permute-start | bytes 1179656 | tf_op jit(solution)/shard_map/ppermute | solution.py:206
  17.6 20.7 %all-to-all-start = ((s32[16,2,256]{2,1,0:T(2,128)}), s32[16,2,256]{2,1,0:T(2,128)S(1)}, u32[]{:S(2)}, u32[]{:S(2)}) async-start(s32[16,2,256]{2,1,0:T(2,128)} %pad_add_fusion), calls=%async_computation | async-start | bytes 65536 | tf_op jit(solution)/shard_map/all_to_all | solution.py:154
  39.7 20.1 %all-to-all-start.1 = ((f32[16,3,4,256]{3,2,1,0:T(4,128)}), f32[16,3,4,256]{3,2,1,0:T(4,128)S(1)}, u32[]{:S(2)}, u32[]{:S(2)}) async-start(f32[16,3,4,256]{3,2,1,0:T(4,128)} %pad_maximum_fusion), calls=%async_computation.1 | async-start | bytes 393216 | tf_op jit(solution)/shard_map/all_to_all | solution.py:154
  60.0 8.0 %collective-permute-start.3 = (f32[3,4,3]{2,1,0:T(4,128)S(1)}, f32[3,4,3]{2,1,0:T(4,128)S(1)}, u32[]{:S(2)}, u32[]{:S(2)}) collective-permute-start(f32[3,4,3]{2,1,0:T(4,128)S(1)} %get-tuple-element.51), channel_id=1, source_target_pairs={{0,1},{1,2},{2,3},{3,4},{4,5},{5,6},{6,7},{8,9},{9,10},{10,11},{11... | collective-permute-start | bytes 440 | tf_op jit(solution)/shard_map/ppermute | solution.py:160
  66.1 4.9 %collective-permute-start.4 = (f32[3,4,3]{2,1,0:T(4,128)S(1)}, f32[3,4,3]{2,1,0:T(4,128)S(1)}, u32[]{:S(2)}, u32[]{:S(2)}) collective-permute-start(f32[3,4,3]{2,1,0:T(4,128)S(1)} %get-tuple-element.52), channel_id=1, source_target_pairs={{1,0},{2,1},{3,2},{4,3},{5,4},{6,5},{7,6},{9,8},{10,9},{11,10},{12... | collective-permute-start | bytes 440 | tf_op jit(solution)/shard_map/ppermute | solution.py:160
  71.1 5.3 %collective-permute-start.5 = (f32[3,3,262]{2,1,0:T(4,128)S(1)}, f32[3,3,262]{2,1,0:T(4,128)S(1)}, u32[]{:S(2)}, u32[]{:S(2)}) collective-permute-start(f32[3,3,262]{2,1,0:T(4,128)S(1)} %get-tuple-element.49), channel_id=1, source_target_pairs={{0,16},{8,24},{16,32},{24,40},{32,48},{40,56},{48,64},{56,72},{64,... | collective-permute-start | bytes 28304 | tf_op jit(solution)/shard_map/ppermute | solution.py:160
  75.1 5.9 %collective-permute-start.6 = (f32[3,3,262]{2,1,0:T(4,128)S(1)}, f32[3,3,262]{2,1,0:T(4,128)S(1)}, u32[]{:S(2)}, u32[]{:S(2)}) collective-permute-start(f32[3,3,262]{2,1,0:T(4,128)S(1)} %get-tuple-element.50), channel_id=1, source_target_pairs={{16,0},{24,8},{32,16},{40,24},{48,32},{56,40},{64,48},{72,56},{80,... | collective-permute-start | bytes 28304 | tf_op jit(solution)/shard_map/ppermute | solution.py:160

commit v3 on v2

--- a/solution.py
+++ b/solution.py
@@ -13,6 +13,7 @@
 STEP_TV = 0.2
 CLASSES = 4
 TM = ("x", "z")
+FIRST_Z = 12
 
 
 def angle_table(freqs, times, total):
@@ -147,12 +148,42 @@
     )(place, weights, frames)
 
 
+def choose_kernel(codes_ref, *refs):
+    *sums_refs, out_ref = refs
+    kinds, rows, cols = sums_refs[0].shape
+    half = cols // 2
+    params = kinds // CLASSES
+    targets, planes, pair, _ = out_ref.shape
+    shown = targets * pair // rows
+    for plane in range(planes):
+        first = plane // params * half
+        level = codes_ref[:, first : first + half] & (CLASSES - 1)
+        own = None
+        for kind in range(CLASSES):
+            at = (kind * params + plane % params, slice(None), slice(first, first + half))
+            total = (sums_refs[0][at] + sums_refs[1][at]) + (sums_refs[2][at] + sums_refs[3][at])
+            own = total if own is None else jnp.where(level == kind, total, own)
+        for target in range(targets):
+            begin = (target + FIRST_Z) % targets // shown * pair
+            out_ref[target, plane] = own[begin : begin + pair]
+
+
+def choose(codes, sums, targets, pair):
+    kinds, _, cols = sums[0].shape
+    vmem = pl.BlockSpec(memory_space=pltpu.VMEM)
+    planes = 2 * (kinds // CLASSES)
+    return pl.pallas_call(
+        choose_kernel,
+        out_shape=jax.ShapeDtypeStruct((targets, planes, pair, cols // 2), jnp.float32),
+        in_specs=[vmem] * (1 + len(sums)),
+        out_specs=vmem,
+        compiler_params=pltpu.CompilerParams(vmem_limit_bytes=32 * 1024 * 1024),
+    )(codes, *sums)
+
+
 def exchange(block, count):
-    middle = count // 2
-    order = [(middle + i) % count for i in range(count)]
-    block = jnp.concatenate([block[middle:], block[:middle]])
-    got = lax.all_to_all(block, "z", 0, 0, axis_index_groups=[order], tiled=True)
-    return jnp.concatenate([got[count - middle :], got[: count - middle]])
+    order = [(FIRST_Z + i) % count for i in range(count)]
+    return lax.all_to_all(block, "z", 0, 0, axis_index_groups=[order], tiled=True)
 
 
 def shifted(block, axis, count, by):
@@ -189,8 +220,11 @@
     x_here = lax.axis_index("x")
     tm_here = lax.axis_index(TM)
 
+    pair = 2 * tile_rows
     codes = classes + CLASSES * valid
-    classes_z = exchange(jnp.broadcast_to(codes[None], (z_devs, *codes.shape)), z_devs)
+    codes = exchange(jnp.broadcast_to(codes[None], (z_devs, *codes.shape)), z_devs)
+    codes = jnp.concatenate([codes[z_devs - FIRST_Z :], codes[: z_devs - FIRST_Z]])
+    codes = codes.reshape(-1, tile_cols)
 
     start, offset, rows = class_system(freqs, total_frames)
     times_here = tm_here * frame_count + jnp.arange(frame_count, dtype=jnp.int32)
@@ -200,24 +234,14 @@
     place = jnp.full((1,), x_here, jnp.int32)
     sums = project(place, split_terms(weights), frames, x_devs)
 
-    total = sums[0]
+    parts = [sums[0]]
     for shift in range(1, x_devs):
         pairs = [(i, (i + shift) % x_devs) for i in range(x_devs)]
-        total = total + lax.ppermute(sums[shift], "x", pairs)
-    pair = 2 * tile_rows
-    total = total.reshape(CLASSES, 3, z_devs // 2, pair, tile_cols)
-    levels = classes_z.reshape(z_devs // 2, pair, tile_cols) % CLASSES
-    own = jnp.zeros(total.shape[1:], jnp.float32)
-    for level in range(CLASSES):
-        own = jnp.where((levels == level)[None], total[level], own)
-    own = jnp.transpose(own, (1, 0, 2, 3))
-    own = jnp.broadcast_to(own[:, None], (z_devs // 2, 2, *own.shape[1:]))
-    own = own.reshape(z_devs, 3, pair, tile_cols)
-    own = exchange(own, z_devs)
-    delta = jnp.sum(own, axis=0)
-    codes = lax.dynamic_index_in_dim(
-        classes_z.reshape(z_devs // 2, pair, tile_cols), lax.axis_index("z") // 2, 0, False
-    )
+        parts.append(lax.ppermute(sums[shift], "x", pairs))
+    own = choose(codes, parts, z_devs, pair)
+    own = jnp.sum(exchange(own, z_devs), axis=0)
+    delta = jnp.concatenate([own[:3], own[3:]], axis=2)
+    codes = lax.dynamic_slice_in_dim(codes, lax.axis_index("z") // 2 * pair, pair, 0)
     classes = codes % CLASSES
     here = start_params(classes)
     base = jnp.zeros_like(here)

time: 82.9 us -> 81.5 us (0.983)
  starting transfers between devices: 55.4 us -> 47.5 us
  waiting for transfers between devices: 17.2 us -> 24.1 us
  other arithmetic: 5.35 us -> 3.78 us
    all_to_all x2, starting transfers between devices: 30.8 us -> 22.8 us  [exchange(): lax.all_to_all(block, 'z', 0, 0, axis_index_groups=[order], tiled=True)]
    all_to_all x2, waiting for transfers between devices: 9.65 us -> 17 us  [exchange(): lax.all_to_all(block, 'z', 0, 0, axis_index_groups=[order], tiled=True)]
    concatenate x3 -> x1, other arithmetic: 1.34 us -> 0.01 us  [on_device(): jnp.concatenate([codes[z_devs - FIRST_Z:], codes[:z_devs - FIRST_Z]])]
where the time goes in v3:
time: 81.5 us; the launch traced here: 81 us
  starting transfers between devices  47.5 us (58%)
  waiting for transfers between devices  24.1 us (30%)
  other arithmetic  3.78 us (5%)
  local copies, waits for them, and re-layouts  2.79 us (3%)
  Pallas kernels  2.41 us (3%)
    all_to_all x2, starting transfers between devices, exchange(): lax.all_to_all(block, 'z', 0, 0, axis_index_groups=[order], tiled=True)  22.8 us
    all_to_all x2, waiting for transfers between devices, exchange(): lax.all_to_all(block, 'z', 0, 0, axis_index_groups=[order], tiled=True)  17 us
    ppermute x4, starting transfers between devices, shifted(): return lax.ppermute(block, axis, pairs)  13.4 us
    ppermute x3, starting transfers between devices, on_device(): parts.append(lax.ppermute(sums[shift], 'x', pairs))  11.4 us
    ppermute x4, waiting for transfers between devices, shifted(): return lax.ppermute(block, axis, pairs)  7.08 us
  transfers between devices with their start and end apart: 9, of which 4 were waited for; matrix products, arithmetic and copies ran while one was open for 1% of the time, Pallas kernels for 0%

profile of v3, /device:TPU:1, one launch (start us, length us, event | category | flops | bytes accessed | tf_op | source)
XLA Modules:
  0.0 81.0 jit_solution(3056166217138393005)
XLA Ops:
  0.0 0.7 multiply_sqrt_fusion
  0.7 0.1 add_multiply_fusion.3
  1.0 0.1 multiply_reduce_fusion.2
  1.2 0.1 multiply_reduce_fusion.1
  1.4 0.8 cosine_convert_fusion
  2.2 0.1 multiply_reduce_fusion
  2.4 1.6 %copy-done = bf16[32,128,256]{2,1,0:T(8,128)(2,1)S(1)} copy-done((bf16[32,128,256]{2,1,0:T(8,128)(2,1)S(1)}, bf16[32,128,256]{2,1,0:T(8,128)(2,1)}, u32[]{:S(2)}) %copy-start) | copy-done | bytes 2097176
  3.9 1.6 %shard_map.46 = (f32[12,32,256]{2,1,0:T(8,128)S(1)}, f32[12,32,256]{2,1,0:T(8,128)S(1)}, f32[12,32,256]{2,1,0:T(8,128)S(1)}, f32[12,32,256]{2,1,0:T(8,128)S(1)}) custom-call(s32[1]{0:T(128)} %bitcast.3.place_ref, bf16[36,32]{1,0:T(8,128)(2,1)S(1)} %pad_maximum_fusion.2.weights_ref, bf16[32,128,256]{2,1,0:T(8,128)(2,1)S(1)} %copy-done), custom_call_target="tpu_custom_call" | custom-call | flops 1207959552 | bytes 3670016 | tf_op jit(solution)/shard_map/pallas_call | solution.py:137
  5.6 3.9 %collective-permute-start = (f32[12,32,256]{2,1,0:T(8,128)S(1)}, f32[12,32,256]{2,1,0:T(8,128)S(1)}, u32[]{:S(2)}, u32[]{:S(2)}) collective-permute-start(f32[12,32,256]{2,1,0:T(8,128)S(1)} %get-tuple-element.10), channel_id=1, source_target_pairs={{0,128},{128,256},{256,384},{384,0},{1,129},{129,257},{257,385},{3... | collective-permute-start | bytes 1179656 | tf_op jit(solution)/shard_map/ppermute | solution.py:240
  9.5 4.4 %collective-permute-start.1 = (f32[12,32,256]{2,1,0:T(8,128)S(1)}, f32[12,32,256]{2,1,0:T(8,128)S(1)}, u32[]{:S(2)}, u32[]{:S(2)}) collective-permute-start(f32[12,32,256]{2,1,0:T(8,128)S(1)} %get-tuple-element.11), channel_id=1, source_target_pairs={{0,256},{128,384},{256,0},{384,128},{1,257},{129,385},{257,1},{385... | collective-permute-start | bytes 1179656 | tf_op jit(solution)/shard_map/ppermute | solution.py:240
  13.9 3.1 %collective-permute-start.2 = (f32[12,32,256]{2,1,0:T(8,128)S(1)}, f32[12,32,256]{2,1,0:T(8,128)S(1)}, u32[]{:S(2)}, u32[]{:S(2)}) collective-permute-start(f32[12,32,256]{2,1,0:T(8,128)S(1)} %get-tuple-element.12), channel_id=1, source_target_pairs={{0,384},{128,0},{256,128},{384,256},{1,385},{129,1},{257,129},{385... | collective-permute-start | bytes 1179656 | tf_op jit(solution)/shard_map/ppermute | solution.py:240
  17.0 0.6 broadcast_in_dim.148
  17.6 15.1 %all-to-all-start = ((s32[16,2,256]{2,1,0:T(2,128)}), s32[16,2,256]{2,1,0:T(2,128)S(1)}, u32[]{:S(2)}, u32[]{:S(2)}) async-start(s32[16,2,256]{2,1,0:T(2,128)} %broadcast_in_dim.148), calls=%async_computation | async-start | bytes 65536 | tf_op jit(solution)/shard_map/all_to_all | solution.py:186
  32.8 7.1 %all-to-all-done = s32[16,2,256]{2,1,0:T(2,128)S(1)} async-done(((s32[16,2,256]{2,1,0:T(2,128)}), s32[16,2,256]{2,1,0:T(2,128)S(1)}, u32[]{:S(2)}, u32[]{:S(2)}) %all-to-all-start) | async-done | bytes 32800 | tf_op jit(solution)/shard_map/all_to_all | solution.py:186
  40.0 0.8 shard_map.47
  40.8 7.7 %all-to-all-start.1 = ((f32[16,6,4,128]{3,2,1,0:T(4,128)}), f32[16,6,4,128]{3,2,1,0:T(4,128)S(1)}, u32[]{:S(2)}, u32[]{:S(2)}) async-start(f32[16,6,4,128]{3,2,1,0:T(4,128)} %shard_map.47), calls=%async_computation.1 | async-start | bytes 393216 | tf_op jit(solution)/shard_map/all_to_all | solution.py:186
  48.5 0.2 slice_reduce_fusion.3
  48.8 9.9 %all-to-all-done.1 = f32[16,6,4,128]{3,2,1,0:T(4,128)S(1)} async-done(((f32[16,6,4,128]{3,2,1,0:T(4,128)}), f32[16,6,4,128]{3,2,1,0:T(4,128)S(1)}, u32[]{:S(2)}, u32[]{:S(2)}) %all-to-all-start.1) | async-done | bytes 196640 | tf_op jit(solution)/shard_map/all_to_all | solution.py:186
  58.7 0.1 add_select_fusion
  58.9 7.2 %collective-permute-start.3 = (f32[3,4,3]{2,1,0:T(4,128)S(1)}, f32[3,4,3]{2,1,0:T(4,128)S(1)}, u32[]{:S(2)}, u32[]{:S(2)}) collective-permute-start(f32[3,4,3]{2,1,0:T(4,128)S(1)} %get-tuple-element.36), channel_id=1, source_target_pairs={{0,1},{1,2},{2,3},{3,4},{4,5},{5,6},{6,7},{8,9},{9,10},{10,11},{11... | collective-permute-start | bytes 440 | tf_op jit(solution)/shard_map/ppermute | solution.py:191
  66.1 1.9 %collective-permute-start.4 = (f32[3,4,3]{2,1,0:T(4,128)S(1)}, f32[3,4,3]{2,1,0:T(4,128)S(1)}, u32[]{:S(2)}, u32[]{:S(2)}) collective-permute-start(f32[3,4,3]{2,1,0:T(4,128)S(1)} %get-tuple-element.37), channel_id=1, source_target_pairs={{1,0},{2,1},{3,2},{4,3},{5,4},{6,5},{7,6},{9,8},{10,9},{11,10},{12... | collective-permute-start | bytes 440 | tf_op jit(solution)/shard_map/ppermute | solution.py:191
  68.0 3.0 %collective-permute-done.4 = f32[3,4,3]{2,1,0:T(4,128)S(1)} collective-permute-done((f32[3,4,3]{2,1,0:T(4,128)S(1)}, f32[3,4,3]{2,1,0:T(4,128)S(1)}, u32[]{:S(2)}, u32[]{:S(2)}) %collective-permute-start.4) | collective-permute-done | bytes 176 | tf_op jit(solution)/shard_map/ppermute | solution.py:191
  71.1 2.9 %collective-permute-start.5 = (f32[3,3,262]{2,1,0:T(4,128)S(1)}, f32[3,3,262]{2,1,0:T(4,128)S(1)}, u32[]{:S(2)}, u32[]{:S(2)}) collective-permute-start(f32[3,3,262]{2,1,0:T(4,128)S(1)} %get-tuple-element.34), channel_id=1, source_target_pairs={{0,16},{8,24},{16,32},{24,40},{32,48},{40,56},{48,64},{56,72},{64,... | collective-permute-start | bytes 28304 | tf_op jit(solution)/shard_map/ppermute | solution.py:191
  74.1 1.3 %collective-permute-start.6 = (f32[3,3,262]{2,1,0:T(4,128)S(1)}, f32[3,3,262]{2,1,0:T(4,128)S(1)}, u32[]{:S(2)}, u32[]{:S(2)}) collective-permute-start(f32[3,3,262]{2,1,0:T(4,128)S(1)} %get-tuple-element.35), channel_id=1, source_target_pairs={{16,0},{24,8},{32,16},{40,24},{48,32},{56,40},{64,48},{72,56},{80,... | collective-permute-start | bytes 28304 | tf_op jit(solution)/shard_map/ppermute | solution.py:191
  75.4 4.1 %collective-permute-done.6 = f32[3,3,262]{2,1,0:T(4,128)S(1)} collective-permute-done((f32[3,3,262]{2,1,0:T(4,128)S(1)}, f32[3,3,262]{2,1,0:T(4,128)S(1)}, u32[]{:S(2)}, u32[]{:S(2)}) %collective-permute-start.6) | collective-permute-done | bytes 9464 | tf_op jit(solution)/shard_map/ppermute | solution.py:191
  79.5 0.1 pad_maximum_fusion
  79.6 0.1 fusion.3
  79.7 0.1 fusion.13
  79.8 0.1 fusion.17
  79.9 0.1 fusion.8
  80.1 0.1 fusion.15
  80.4 0.6 fusion.25
  (53 shorter events, 0.9 us)
Async XLA Ops:
  2.3 1.6 %copy-start = (bf16[32,128,256]{2,1,0:T(8,128)(2,1)S(1)}, bf16[32,128,256]{2,1,0:T(8,128)(2,1)}, u32[]{:S(2)}) copy-start(bf16[32,128,256]{2,1,0:T(8,128)(2,1)} %frames_ref.1) | copy-start | bytes 6291460
  3.9 13.0 %copy-start.1 = (s32[2,256]{1,0:T(2,128)S(1)}, s32[2,256]{1,0:T(2,128)}, u32[]{:S(2)}) copy-start(s32[2,256]{1,0:T(2,128)} %param.7) | copy-start | bytes 6148
  3.9 13.0 %copy-start.2 = (s32[2,256]{1,0:T(2,128)S(1)}, s32[2,256]{1,0:T(2,128)}, u32[]{:S(2)}) copy-start(s32[2,256]{1,0:T(2,128)} %param.6) | copy-start | bytes 6148
  5.6 34.4 %collective-permute-start = (f32[12,32,256]{2,1,0:T(8,128)S(1)}, f32[12,32,256]{2,1,0:T(8,128)S(1)}, u32[]{:S(2)}, u32[]{:S(2)}) collective-permute-start(f32[12,32,256]{2,1,0:T(8,128)S(1)} %get-tuple-element.10), channel_id=1, source_target_pairs={{0,128},{128,256},{256,384},{384,0},{1,129},{129,257},{257,385},{3... | collective-permute-start | bytes 1179656 | tf_op jit(solution)/shard_map/ppermute | solution.py:240
  9.5 30.4 %collective-permute-start.1 = (f32[12,32,256]{2,1,0:T(8,128)S(1)}, f32[12,32,256]{2,1,0:T(8,128)S(1)}, u32[]{:S(2)}, u32[]{:S(2)}) collective-permute-start(f32[12,32,256]{2,1,0:T(8,128)S(1)} %get-tuple-element.11), channel_id=1, source_target_pairs={{0,256},{128,384},{256,0},{384,128},{1,257},{129,385},{257,1},{385... | collective-permute-start | bytes 1179656 | tf_op jit(solution)/shard_map/ppermute | solution.py:240
  13.9 26.1 %collective-permute-start.2 = (f32[12,32,256]{2,1,0:T(8,128)S(1)}, f32[12,32,256]{2,1,0:T(8,128)S(1)}, u32[]{:S(2)}, u32[]{:S(2)}) collective-permute-start(f32[12,32,256]{2,1,0:T(8,128)S(1)} %get-tuple-element.12), channel_id=1, source_target_pairs={{0,384},{128,0},{256,128},{384,256},{1,385},{129,1},{257,129},{385... | collective-permute-start | bytes 1179656 | tf_op jit(solution)/shard_map/ppermute | solution.py:240
  17.6 22.3 %all-to-all-start = ((s32[16,2,256]{2,1,0:T(2,128)}), s32[16,2,256]{2,1,0:T(2,128)S(1)}, u32[]{:S(2)}, u32[]{:S(2)}) async-start(s32[16,2,256]{2,1,0:T(2,128)} %broadcast_in_dim.148), calls=%async_computation | async-start | bytes 65536 | tf_op jit(solution)/shard_map/all_to_all | solution.py:186
  40.8 17.9 %all-to-all-start.1 = ((f32[16,6,4,128]{3,2,1,0:T(4,128)}), f32[16,6,4,128]{3,2,1,0:T(4,128)S(1)}, u32[]{:S(2)}, u32[]{:S(2)}) async-start(f32[16,6,4,128]{3,2,1,0:T(4,128)} %shard_map.47), calls=%async_computation.1 | async-start | bytes 393216 | tf_op jit(solution)/shard_map/all_to_all | solution.py:186
  58.9 9.1 %collective-permute-start.3 = (f32[3,4,3]{2,1,0:T(4,128)S(1)}, f32[3,4,3]{2,1,0:T(4,128)S(1)}, u32[]{:S(2)}, u32[]{:S(2)}) collective-permute-start(f32[3,4,3]{2,1,0:T(4,128)S(1)} %get-tuple-element.36), channel_id=1, source_target_pairs={{0,1},{1,2},{2,3},{3,4},{4,5},{5,6},{6,7},{8,9},{9,10},{10,11},{11... | collective-permute-start | bytes 440 | tf_op jit(solution)/shard_map/ppermute | solution.py:191
  66.1 4.9 %collective-permute-start.4 = (f32[3,4,3]{2,1,0:T(4,128)S(1)}, f32[3,4,3]{2,1,0:T(4,128)S(1)}, u32[]{:S(2)}, u32[]{:S(2)}) collective-permute-start(f32[3,4,3]{2,1,0:T(4,128)S(1)} %get-tuple-element.37), channel_id=1, source_target_pairs={{1,0},{2,1},{3,2},{4,3},{5,4},{6,5},{7,6},{9,8},{10,9},{11,10},{12... | collective-permute-start | bytes 440 | tf_op jit(solution)/shard_map/ppermute | solution.py:191
  71.1 4.3 %collective-permute-start.5 = (f32[3,3,262]{2,1,0:T(4,128)S(1)}, f32[3,3,262]{2,1,0:T(4,128)S(1)}, u32[]{:S(2)}, u32[]{:S(2)}) collective-permute-start(f32[3,3,262]{2,1,0:T(4,128)S(1)} %get-tuple-element.34), channel_id=1, source_target_pairs={{0,16},{8,24},{16,32},{24,40},{32,48},{40,56},{48,64},{56,72},{64,... | collective-permute-start | bytes 28304 | tf_op jit(solution)/shard_map/ppermute | solution.py:191
  74.1 5.4 %collective-permute-start.6 = (f32[3,3,262]{2,1,0:T(4,128)S(1)}, f32[3,3,262]{2,1,0:T(4,128)S(1)}, u32[]{:S(2)}, u32[]{:S(2)}) collective-permute-start(f32[3,3,262]{2,1,0:T(4,128)S(1)} %get-tuple-element.35), channel_id=1, source_target_pairs={{16,0},{24,8},{32,16},{40,24},{48,32},{56,40},{64,48},{72,56},{80,... | collective-permute-start | bytes 28304 | tf_op jit(solution)/shard_map/ppermute | solution.py:191

commit v4 on v3

--- a/solution.py
+++ b/solution.py
@@ -13,7 +13,7 @@
 STEP_TV = 0.2
 CLASSES = 4
 TM = ("x", "z")
-FIRST_Z = 12
+FIRST_Z = 11
 
 
 def angle_table(freqs, times, total):
@@ -235,7 +235,7 @@
     sums = project(place, split_terms(weights), frames, x_devs)
 
     parts = [sums[0]]
-    for shift in range(1, x_devs):
+    for shift in (1, 3, 2):
         pairs = [(i, (i + shift) % x_devs) for i in range(x_devs)]
         parts.append(lax.ppermute(sums[shift], "x", pairs))
     own = choose(codes, parts, z_devs, pair)

time: 81.5 us -> 79.4 us (0.974)
  waiting for transfers between devices: 24.1 us -> 21.1 us
  starting transfers between devices: 47.5 us -> 48.4 us
    all_to_all x2, waiting for transfers between devices: 17 us -> 14 us  [exchange(): lax.all_to_all(block, 'z', 0, 0, axis_index_groups=[order], tiled=True)]
    all_to_all x2, starting transfers between devices: 22.8 us -> 25.2 us  [exchange(): lax.all_to_all(block, 'z', 0, 0, axis_index_groups=[order], tiled=True)]
    ppermute x4, starting transfers between devices: 13.4 us -> 12.5 us  [shifted(): return lax.ppermute(block, axis, pairs)]
where the time goes in v4:
time: 79.4 us; the launch traced here: 78.9 us
  starting transfers between devices  48.4 us (61%)
  waiting for transfers between devices  21.1 us (27%)
  other arithmetic  3.78 us (5%)
  local copies, waits for them, and re-layouts  2.79 us (4%)
  Pallas kernels  2.41 us (3%)
    all_to_all x2, starting transfers between devices, exchange(): lax.all_to_all(block, 'z', 0, 0, axis_index_groups=[order], tiled=True)  25.2 us
    all_to_all x2, waiting for transfers between devices, exchange(): lax.all_to_all(block, 'z', 0, 0, axis_index_groups=[order], tiled=True)  14 us
    ppermute x4, starting transfers between devices, shifted(): return lax.ppermute(block, axis, pairs)  12.5 us
    ppermute x3, starting transfers between devices, on_device(): parts.append(lax.ppermute(sums[shift], 'x', pairs))  10.8 us
    ppermute x4, waiting for transfers between devices, shifted(): return lax.ppermute(block, axis, pairs)  7.08 us
    pallas_call x1, Pallas kernels, project(): pl.pallas_call(project_kernel, out_shape=[out] * parts, in_specs=[pl.Bloc...  1.63 us
    unnamed x7, local copies, waits for them, and re-layouts  1.6 us
  transfers between devices with their start and end apart: 9, of which 4 were waited for; matrix products, arithmetic and copies ran while one was open for 1% of the time, Pallas kernels for 0%

profile of v4, /device:TPU:1, one launch (start us, length us, event | category | flops | bytes accessed | tf_op | source)
XLA Modules:
  0.0 78.9 jit_solution(5160752275363922084)
XLA Ops:
  0.0 0.7 multiply_sqrt_fusion
  0.7 0.1 add_multiply_fusion.3
  1.0 0.1 multiply_reduce_fusion.2
  1.2 0.1 multiply_reduce_fusion.1
  1.4 0.8 cosine_convert_fusion
  2.2 0.1 multiply_reduce_fusion
  2.4 1.6 %copy-done = bf16[32,128,256]{2,1,0:T(8,128)(2,1)S(1)} copy-done((bf16[32,128,256]{2,1,0:T(8,128)(2,1)S(1)}, bf16[32,128,256]{2,1,0:T(8,128)(2,1)}, u32[]{:S(2)}) %copy-start) | copy-done | bytes 2097176
  3.9 1.6 %shard_map.46 = (f32[12,32,256]{2,1,0:T(8,128)S(1)}, f32[12,32,256]{2,1,0:T(8,128)S(1)}, f32[12,32,256]{2,1,0:T(8,128)S(1)}, f32[12,32,256]{2,1,0:T(8,128)S(1)}) custom-call(s32[1]{0:T(128)} %bitcast.3.place_ref, bf16[36,32]{1,0:T(8,128)(2,1)S(1)} %pad_maximum_fusion.2.weights_ref, bf16[32,128,256]{2,1,0:T(8,128)(2,1)S(1)} %copy-done), custom_call_target="tpu_custom_call" | custom-call | flops 1207959552 | bytes 3670016 | tf_op jit(solution)/shard_map/pallas_call | solution.py:137
  5.6 3.9 %collective-permute-start = (f32[12,32,256]{2,1,0:T(8,128)S(1)}, f32[12,32,256]{2,1,0:T(8,128)S(1)}, u32[]{:S(2)}, u32[]{:S(2)}) collective-permute-start(f32[12,32,256]{2,1,0:T(8,128)S(1)} %get-tuple-element.10), channel_id=1, source_target_pairs={{0,128},{128,256},{256,384},{384,0},{1,129},{129,257},{257,385},{3... | collective-permute-start | bytes 1179656 | tf_op jit(solution)/shard_map/ppermute | solution.py:240
  9.5 3.2 %collective-permute-start.1 = (f32[12,32,256]{2,1,0:T(8,128)S(1)}, f32[12,32,256]{2,1,0:T(8,128)S(1)}, u32[]{:S(2)}, u32[]{:S(2)}) collective-permute-start(f32[12,32,256]{2,1,0:T(8,128)S(1)} %get-tuple-element.11), channel_id=1, source_target_pairs={{0,384},{128,0},{256,128},{384,256},{1,385},{129,1},{257,129},{385... | collective-permute-start | bytes 1179656 | tf_op jit(solution)/shard_map/ppermute | solution.py:240
  12.7 3.6 %collective-permute-start.2 = (f32[12,32,256]{2,1,0:T(8,128)S(1)}, f32[12,32,256]{2,1,0:T(8,128)S(1)}, u32[]{:S(2)}, u32[]{:S(2)}) collective-permute-start(f32[12,32,256]{2,1,0:T(8,128)S(1)} %get-tuple-element.12), channel_id=1, source_target_pairs={{0,256},{128,384},{256,0},{384,128},{1,257},{129,385},{257,1},{385... | collective-permute-start | bytes 1179656 | tf_op jit(solution)/shard_map/ppermute | solution.py:240
  16.4 0.6 broadcast_in_dim.148
  17.0 15.6 %all-to-all-start = ((s32[16,2,256]{2,1,0:T(2,128)}), s32[16,2,256]{2,1,0:T(2,128)S(1)}, u32[]{:S(2)}, u32[]{:S(2)}) async-start(s32[16,2,256]{2,1,0:T(2,128)} %broadcast_in_dim.148), calls=%async_computation | async-start | bytes 65536 | tf_op jit(solution)/shard_map/all_to_all | solution.py:186
  32.7 5.0 %all-to-all-done = s32[16,2,256]{2,1,0:T(2,128)S(1)} async-done(((s32[16,2,256]{2,1,0:T(2,128)}), s32[16,2,256]{2,1,0:T(2,128)S(1)}, u32[]{:S(2)}, u32[]{:S(2)}) %all-to-all-start) | async-done | bytes 32800 | tf_op jit(solution)/shard_map/all_to_all | solution.py:186
  37.8 0.8 shard_map.47
  38.6 9.6 %all-to-all-start.1 = ((f32[16,6,4,128]{3,2,1,0:T(4,128)}), f32[16,6,4,128]{3,2,1,0:T(4,128)S(1)}, u32[]{:S(2)}, u32[]{:S(2)}) async-start(f32[16,6,4,128]{3,2,1,0:T(4,128)} %shard_map.47), calls=%async_computation.1 | async-start | bytes 393216 | tf_op jit(solution)/shard_map/all_to_all | solution.py:186
  48.2 0.2 slice_reduce_fusion.3
  48.5 9.0 %all-to-all-done.1 = f32[16,6,4,128]{3,2,1,0:T(4,128)S(1)} async-done(((f32[16,6,4,128]{3,2,1,0:T(4,128)}), f32[16,6,4,128]{3,2,1,0:T(4,128)S(1)}, u32[]{:S(2)}, u32[]{:S(2)}) %all-to-all-start.1) | async-done | bytes 196640 | tf_op jit(solution)/shard_map/all_to_all | solution.py:186
  57.5 0.1 add_select_fusion
  57.7 6.9 %collective-permute-start.3 = (f32[3,4,3]{2,1,0:T(4,128)S(1)}, f32[3,4,3]{2,1,0:T(4,128)S(1)}, u32[]{:S(2)}, u32[]{:S(2)}) collective-permute-start(f32[3,4,3]{2,1,0:T(4,128)S(1)} %get-tuple-element.36), channel_id=1, source_target_pairs={{0,1},{1,2},{2,3},{3,4},{4,5},{5,6},{6,7},{8,9},{9,10},{10,11},{11... | collective-permute-start | bytes 440 | tf_op jit(solution)/shard_map/ppermute | solution.py:191
  64.6 1.9 %collective-permute-start.4 = (f32[3,4,3]{2,1,0:T(4,128)S(1)}, f32[3,4,3]{2,1,0:T(4,128)S(1)}, u32[]{:S(2)}, u32[]{:S(2)}) collective-permute-start(f32[3,4,3]{2,1,0:T(4,128)S(1)} %get-tuple-element.37), channel_id=1, source_target_pairs={{1,0},{2,1},{3,2},{4,3},{5,4},{6,5},{7,6},{9,8},{10,9},{11,10},{12... | collective-permute-start | bytes 440 | tf_op jit(solution)/shard_map/ppermute | solution.py:191
  66.6 3.0 %collective-permute-done.4 = f32[3,4,3]{2,1,0:T(4,128)S(1)} collective-permute-done((f32[3,4,3]{2,1,0:T(4,128)S(1)}, f32[3,4,3]{2,1,0:T(4,128)S(1)}, u32[]{:S(2)}, u32[]{:S(2)}) %collective-permute-start.4) | collective-permute-done | bytes 176 | tf_op jit(solution)/shard_map/ppermute | solution.py:191
  69.7 2.3 %collective-permute-start.5 = (f32[3,3,262]{2,1,0:T(4,128)S(1)}, f32[3,3,262]{2,1,0:T(4,128)S(1)}, u32[]{:S(2)}, u32[]{:S(2)}) collective-permute-start(f32[3,3,262]{2,1,0:T(4,128)S(1)} %get-tuple-element.34), channel_id=1, source_target_pairs={{0,16},{8,24},{16,32},{24,40},{32,48},{40,56},{48,64},{56,72},{64,... | collective-permute-start | bytes 28304 | tf_op jit(solution)/shard_map/ppermute | solution.py:191
  72.0 1.3 %collective-permute-start.6 = (f32[3,3,262]{2,1,0:T(4,128)S(1)}, f32[3,3,262]{2,1,0:T(4,128)S(1)}, u32[]{:S(2)}, u32[]{:S(2)}) collective-permute-start(f32[3,3,262]{2,1,0:T(4,128)S(1)} %get-tuple-element.35), channel_id=1, source_target_pairs={{16,0},{24,8},{32,16},{40,24},{48,32},{56,40},{64,48},{72,56},{80,... | collective-permute-start | bytes 28304 | tf_op jit(solution)/shard_map/ppermute | solution.py:191
  73.3 4.1 %collective-permute-done.6 = f32[3,3,262]{2,1,0:T(4,128)S(1)} collective-permute-done((f32[3,3,262]{2,1,0:T(4,128)S(1)}, f32[3,3,262]{2,1,0:T(4,128)S(1)}, u32[]{:S(2)}, u32[]{:S(2)}) %collective-permute-start.6) | collective-permute-done | bytes 9464 | tf_op jit(solution)/shard_map/ppermute | solution.py:191
  77.4 0.1 pad_maximum_fusion
  77.5 0.1 fusion.3
  77.6 0.1 fusion.13
  77.8 0.1 fusion.17
  77.9 0.1 fusion.8
  78.1 0.1 fusion.15
  78.3 0.6 fusion.25
  (53 shorter events, 0.9 us)
Async XLA Ops:
  2.3 1.6 %copy-start = (bf16[32,128,256]{2,1,0:T(8,128)(2,1)S(1)}, bf16[32,128,256]{2,1,0:T(8,128)(2,1)}, u32[]{:S(2)}) copy-start(bf16[32,128,256]{2,1,0:T(8,128)(2,1)} %frames_ref.1) | copy-start | bytes 6291460
  3.9 12.4 %copy-start.1 = (s32[2,256]{1,0:T(2,128)S(1)}, s32[2,256]{1,0:T(2,128)}, u32[]{:S(2)}) copy-start(s32[2,256]{1,0:T(2,128)} %param.7) | copy-start | bytes 6148
  3.9 12.4 %copy-start.2 = (s32[2,256]{1,0:T(2,128)S(1)}, s32[2,256]{1,0:T(2,128)}, u32[]{:S(2)}) copy-start(s32[2,256]{1,0:T(2,128)} %param.6) | copy-start | bytes 6148
  5.6 32.2 %collective-permute-start = (f32[12,32,256]{2,1,0:T(8,128)S(1)}, f32[12,32,256]{2,1,0:T(8,128)S(1)}, u32[]{:S(2)}, u32[]{:S(2)}) collective-permute-start(f32[12,32,256]{2,1,0:T(8,128)S(1)} %get-tuple-element.10), channel_id=1, source_target_pairs={{0,128},{128,256},{256,384},{384,0},{1,129},{129,257},{257,385},{3... | collective-permute-start | bytes 1179656 | tf_op jit(solution)/shard_map/ppermute | solution.py:240
  9.5 28.2 %collective-permute-start.1 = (f32[12,32,256]{2,1,0:T(8,128)S(1)}, f32[12,32,256]{2,1,0:T(8,128)S(1)}, u32[]{:S(2)}, u32[]{:S(2)}) collective-permute-start(f32[12,32,256]{2,1,0:T(8,128)S(1)} %get-tuple-element.11), channel_id=1, source_target_pairs={{0,384},{128,0},{256,128},{384,256},{1,385},{129,1},{257,129},{385... | collective-permute-start | bytes 1179656 | tf_op jit(solution)/shard_map/ppermute | solution.py:240
  12.7 25.1 %collective-permute-start.2 = (f32[12,32,256]{2,1,0:T(8,128)S(1)}, f32[12,32,256]{2,1,0:T(8,128)S(1)}, u32[]{:S(2)}, u32[]{:S(2)}) collective-permute-start(f32[12,32,256]{2,1,0:T(8,128)S(1)} %get-tuple-element.12), channel_id=1, source_target_pairs={{0,256},{128,384},{256,0},{384,128},{1,257},{129,385},{257,1},{385... | collective-permute-start | bytes 1179656 | tf_op jit(solution)/shard_map/ppermute | solution.py:240
  17.0 20.7 %all-to-all-start = ((s32[16,2,256]{2,1,0:T(2,128)}), s32[16,2,256]{2,1,0:T(2,128)S(1)}, u32[]{:S(2)}, u32[]{:S(2)}) async-start(s32[16,2,256]{2,1,0:T(2,128)} %broadcast_in_dim.148), calls=%async_computation | async-start | bytes 65536 | tf_op jit(solution)/shard_map/all_to_all | solution.py:186
  38.6 18.9 %all-to-all-start.1 = ((f32[16,6,4,128]{3,2,1,0:T(4,128)}), f32[16,6,4,128]{3,2,1,0:T(4,128)S(1)}, u32[]{:S(2)}, u32[]{:S(2)}) async-start(f32[16,6,4,128]{3,2,1,0:T(4,128)} %shard_map.47), calls=%async_computation.1 | async-start | bytes 393216 | tf_op jit(solution)/shard_map/all_to_all | solution.py:186
  57.7 8.9 %collective-permute-start.3 = (f32[3,4,3]{2,1,0:T(4,128)S(1)}, f32[3,4,3]{2,1,0:T(4,128)S(1)}, u32[]{:S(2)}, u32[]{:S(2)}) collective-permute-start(f32[3,4,3]{2,1,0:T(4,128)S(1)} %get-tuple-element.36), channel_id=1, source_target_pairs={{0,1},{1,2},{2,3},{3,4},{4,5},{5,6},{6,7},{8,9},{9,10},{10,11},{11... | collective-permute-start | bytes 440 | tf_op jit(solution)/shard_map/ppermute | solution.py:191
  64.6 4.9 %collective-permute-start.4 = (f32[3,4,3]{2,1,0:T(4,128)S(1)}, f32[3,4,3]{2,1,0:T(4,128)S(1)}, u32[]{:S(2)}, u32[]{:S(2)}) collective-permute-start(f32[3,4,3]{2,1,0:T(4,128)S(1)} %get-tuple-element.37), channel_id=1, source_target_pairs={{1,0},{2,1},{3,2},{4,3},{5,4},{6,5},{7,6},{9,8},{10,9},{11,10},{12... | collective-permute-start | bytes 440 | tf_op jit(solution)/shard_map/ppermute | solution.py:191
  69.7 3.7 %collective-permute-start.5 = (f32[3,3,262]{2,1,0:T(4,128)S(1)}, f32[3,3,262]{2,1,0:T(4,128)S(1)}, u32[]{:S(2)}, u32[]{:S(2)}) collective-permute-start(f32[3,3,262]{2,1,0:T(4,128)S(1)} %get-tuple-element.34), channel_id=1, source_target_pairs={{0,16},{8,24},{16,32},{24,40},{32,48},{40,56},{48,64},{56,72},{64,... | collective-permute-start | bytes 28304 | tf_op jit(solution)/shard_map/ppermute | solution.py:191
  72.0 5.4 %collective-permute-start.6 = (f32[3,3,262]{2,1,0:T(4,128)S(1)}, f32[3,3,262]{2,1,0:T(4,128)S(1)}, u32[]{:S(2)}, u32[]{:S(2)}) collective-permute-start(f32[3,3,262]{2,1,0:T(4,128)S(1)} %get-tuple-element.35), channel_id=1, source_target_pairs={{16,0},{24,8},{32,16},{40,24},{48,32},{56,40},{64,48},{72,56},{80,... | collective-permute-start | bytes 28304 | tf_op jit(solution)/shard_map/ppermute | solution.py:191

commit v5 on v4

--- a/solution.py
+++ b/solution.py
@@ -187,7 +187,7 @@
 
 
 def shifted(block, axis, count, by):
-    pairs = [(i, i + by) for i in range(count) if 0 <= i + by < count]
+    pairs = [(i, (i + by) % count) for i in range(count)]
     return lax.ppermute(block, axis, pairs)
 
 

time: 79.4 us -> 78.2 us (0.985)
  waiting for transfers between devices: 21.1 us -> 17.9 us
  starting transfers between devices: 48.4 us -> 50.5 us
    ppermute x4, waiting for transfers between devices: 7.08 us -> 3.88 us  [shifted(): return lax.ppermute(block, axis, pairs)]
    ppermute x4, starting transfers between devices: 12.5 us -> 14.5 us  [shifted(): return lax.ppermute(block, axis, pairs)]
  transfers between devices with their start and end apart: 9 -> 9, of which waited for: 4 -> 5; matrix products, arithmetic and copies ran while one was open for 1% -> 1% of each run, Pallas kernels for 0% -> 0%
where the time goes in v5:
time: 78.2 us; the launch traced here: 77.8 us
  starting transfers between devices  50.5 us (65%)
  waiting for transfers between devices  17.9 us (23%)
  other arithmetic  3.78 us (5%)
  local copies, waits for them, and re-layouts  2.79 us (4%)
  Pallas kernels  2.41 us (3%)
    all_to_all x2, starting transfers between devices, exchange(): lax.all_to_all(block, 'z', 0, 0, axis_index_groups=[order], tiled=True)  25.2 us
    ppermute x4, starting transfers between devices, shifted(): return lax.ppermute(block, axis, pairs)  14.5 us
    all_to_all x2, waiting for transfers between devices, exchange(): lax.all_to_all(block, 'z', 0, 0, axis_index_groups=[order], tiled=True)  14 us
    ppermute x3, starting transfers between devices, on_device(): parts.append(lax.ppermute(sums[shift], 'x', pairs))  10.8 us
    ppermute x4, waiting for transfers between devices, shifted(): return lax.ppermute(block, axis, pairs)  3.88 us
    pallas_call x1, Pallas kernels, project(): pl.pallas_call(project_kernel, out_shape=[out] * parts, in_specs=[pl.Bloc...  1.63 us
    unnamed x7, local copies, waits for them, and re-layouts  1.6 us
  transfers between devices with their start and end apart: 9, of which 5 were waited for; matrix products, arithmetic and copies ran while one was open for 1% of the time, Pallas kernels for 0%

profile of v5, /device:TPU:1, one launch (start us, length us, event | category | flops | bytes accessed | tf_op | source)
XLA Modules:
  0.0 77.8 jit_solution(14883526439815894424)
XLA Ops:
  0.0 0.7 multiply_sqrt_fusion
  0.7 0.1 add_multiply_fusion.3
  1.0 0.1 multiply_reduce_fusion.2
  1.2 0.1 multiply_reduce_fusion.1
  1.4 0.8 %cosine_convert_fusion = (bf16[16,32]{1,0:T(8,128)(2,1)S(1)}, bf16[16,32]{1,0:T(8,128)(2,1)S(1)}) fusion(s32[32]{0:T(128)S(1)} %iota_add_fusion.3, s32[16]{0:T(128)} %param.5), kind=kLoop, calls=%fused_computation.59 | loop fusion | flops 8704 | bytes 2240 | tf_op jit(solution)/shard_map/convert
  2.2 0.1 multiply_reduce_fusion
  2.4 1.6 %copy-done = bf16[32,128,256]{2,1,0:T(8,128)(2,1)S(1)} copy-done((bf16[32,128,256]{2,1,0:T(8,128)(2,1)S(1)}, bf16[32,128,256]{2,1,0:T(8,128)(2,1)}, u32[]{:S(2)}) %copy-start) | copy-done | bytes 2097176
  3.9 1.6 %shard_map.46 = (f32[12,32,256]{2,1,0:T(8,128)S(1)}, f32[12,32,256]{2,1,0:T(8,128)S(1)}, f32[12,32,256]{2,1,0:T(8,128)S(1)}, f32[12,32,256]{2,1,0:T(8,128)S(1)}) custom-call(s32[1]{0:T(128)} %bitcast.3.place_ref, bf16[36,32]{1,0:T(8,128)(2,1)S(1)} %pad_maximum_fusion.2.weights_ref, bf16[32,128,256]{2,1,0:T(8,128)(2,1)S(1)} %copy-done), custom_call_target="tpu_custom_call" | custom-call | flops 1207959552 | bytes 3670016 | tf_op jit(solution)/shard_map/pallas_call | solution.py:137
  5.6 3.9 %collective-permute-start = (f32[12,32,256]{2,1,0:T(8,128)S(1)}, f32[12,32,256]{2,1,0:T(8,128)S(1)}, u32[]{:S(2)}, u32[]{:S(2)}) collective-permute-start(f32[12,32,256]{2,1,0:T(8,128)S(1)} %get-tuple-element.10), channel_id=1, source_target_pairs={{0,128},{128,256},{256,384},{384,0},{1,129},{129,257},{257,385},{3... | collective-permute-start | bytes 1179656 | tf_op jit(solution)/shard_map/ppermute | solution.py:240
  9.5 3.2 %collective-permute-start.1 = (f32[12,32,256]{2,1,0:T(8,128)S(1)}, f32[12,32,256]{2,1,0:T(8,128)S(1)}, u32[]{:S(2)}, u32[]{:S(2)}) collective-permute-start(f32[12,32,256]{2,1,0:T(8,128)S(1)} %get-tuple-element.11), channel_id=1, source_target_pairs={{0,384},{128,0},{256,128},{384,256},{1,385},{129,1},{257,129},{385... | collective-permute-start | bytes 1179656 | tf_op jit(solution)/shard_map/ppermute | solution.py:240
  12.7 3.6 %collective-permute-start.2 = (f32[12,32,256]{2,1,0:T(8,128)S(1)}, f32[12,32,256]{2,1,0:T(8,128)S(1)}, u32[]{:S(2)}, u32[]{:S(2)}) collective-permute-start(f32[12,32,256]{2,1,0:T(8,128)S(1)} %get-tuple-element.12), channel_id=1, source_target_pairs={{0,256},{128,384},{256,0},{384,128},{1,257},{129,385},{257,1},{385... | collective-permute-start | bytes 1179656 | tf_op jit(solution)/shard_map/ppermute | solution.py:240
  16.4 0.6 broadcast_in_dim.148
  17.0 15.6 %all-to-all-start = ((s32[16,2,256]{2,1,0:T(2,128)}), s32[16,2,256]{2,1,0:T(2,128)S(1)}, u32[]{:S(2)}, u32[]{:S(2)}) async-start(s32[16,2,256]{2,1,0:T(2,128)} %broadcast_in_dim.148), calls=%async_computation | async-start | bytes 65536 | tf_op jit(solution)/shard_map/all_to_all | solution.py:186
  32.7 5.0 %all-to-all-done = s32[16,2,256]{2,1,0:T(2,128)S(1)} async-done(((s32[16,2,256]{2,1,0:T(2,128)}), s32[16,2,256]{2,1,0:T(2,128)S(1)}, u32[]{:S(2)}, u32[]{:S(2)}) %all-to-all-start) | async-done | bytes 32800 | tf_op jit(solution)/shard_map/all_to_all | solution.py:186
  37.8 0.8 %shard_map.47 = f32[16,6,4,128]{3,2,1,0:T(4,128)} custom-call(s32[32,256]{1,0:T(8,128)S(1)} %reshape.447.codes_ref, f32[12,32,256]{2,1,0:T(8,128)S(1)} %get-tuple-element.9.refs_0_, f32[12,32,256]{2,1,0:T(8,128)S(1)} %collective-permute-done.refs_1_, f32[12,32,256]{2,1,0:T(8,128)S(1)} %collective-permute-done.1.refs_2_, ...), custom_call_target="tpu_custom_call" | custom-call | tf_op jit(solution)/shard_map/pallas_call | solution.py:175
  38.6 9.6 %all-to-all-start.1 = ((f32[16,6,4,128]{3,2,1,0:T(4,128)}), f32[16,6,4,128]{3,2,1,0:T(4,128)S(1)}, u32[]{:S(2)}, u32[]{:S(2)}) async-start(f32[16,6,4,128]{3,2,1,0:T(4,128)} %shard_map.47), calls=%async_computation.1 | async-start | bytes 393216 | tf_op jit(solution)/shard_map/all_to_all | solution.py:186
  48.2 0.2 slice_reduce_fusion.3
  48.5 9.0 %all-to-all-done.1 = f32[16,6,4,128]{3,2,1,0:T(4,128)S(1)} async-done(((f32[16,6,4,128]{3,2,1,0:T(4,128)}), f32[16,6,4,128]{3,2,1,0:T(4,128)S(1)}, u32[]{:S(2)}, u32[]{:S(2)}) %all-to-all-start.1) | async-done | bytes 196640 | tf_op jit(solution)/shard_map/all_to_all | solution.py:186
  57.5 0.1 add_select_fusion
  57.7 5.0 %collective-permute-start.3 = (f32[3,4,3]{2,1,0:T(4,128)S(1)}, f32[3,4,3]{2,1,0:T(4,128)S(1)}, u32[]{:S(2)}, u32[]{:S(2)}) collective-permute-start(f32[3,4,3]{2,1,0:T(4,128)S(1)} %get-tuple-element.36), channel_id=1, source_target_pairs={{0,1},{1,2},{2,3},{3,4},{4,5},{5,6},{6,7},{7,0},{8,9},{9,10},{10,1... | collective-permute-start | bytes 440 | tf_op jit(solution)/shard_map/ppermute | solution.py:191
  62.7 0.8 collective-permute-done.3
  63.5 2.3 %collective-permute-done.4 = f32[3,4,3]{2,1,0:T(4,128)S(1)} collective-permute-done((f32[3,4,3]{2,1,0:T(4,128)S(1)}, f32[3,4,3]{2,1,0:T(4,128)S(1)}, u32[]{:S(2)}, u32[]{:S(2)}) %collective-permute-start.4) | collective-permute-done | bytes 176 | tf_op jit(solution)/shard_map/ppermute | solution.py:191
  65.9 2.3 %collective-permute-start.5 = (f32[3,3,262]{2,1,0:T(4,128)S(1)}, f32[3,3,262]{2,1,0:T(4,128)S(1)}, u32[]{:S(2)}, u32[]{:S(2)}) collective-permute-start(f32[3,3,262]{2,1,0:T(4,128)S(1)} %get-tuple-element.34), channel_id=1, source_target_pairs={{0,16},{8,24},{16,32},{24,40},{32,48},{40,56},{48,64},{56,72},{64,... | collective-permute-start | bytes 28304 | tf_op jit(solution)/shard_map/ppermute | solution.py:191
  68.2 7.2 %collective-permute-start.6 = (f32[3,3,262]{2,1,0:T(4,128)S(1)}, f32[3,3,262]{2,1,0:T(4,128)S(1)}, u32[]{:S(2)}, u32[]{:S(2)}) collective-permute-start(f32[3,3,262]{2,1,0:T(4,128)S(1)} %get-tuple-element.35), channel_id=1, source_target_pairs={{0,496},{8,504},{16,0},{24,8},{32,16},{40,24},{48,32},{56,40},{64,... | collective-permute-start | bytes 28304 | tf_op jit(solution)/shard_map/ppermute | solution.py:191
  75.4 0.8 %collective-permute-done.6 = f32[3,3,262]{2,1,0:T(4,128)S(1)} collective-permute-done((f32[3,3,262]{2,1,0:T(4,128)S(1)}, f32[3,3,262]{2,1,0:T(4,128)S(1)}, u32[]{:S(2)}, u32[]{:S(2)}) %collective-permute-start.6) | collective-permute-done | bytes 9464 | tf_op jit(solution)/shard_map/ppermute | solution.py:191
  76.2 0.1 pad_maximum_fusion
  76.3 0.1 fusion.3
  76.5 0.1 fusion.13
  76.6 0.1 fusion.17
  76.7 0.1 fusion.8
  76.9 0.1 fusion.15
  77.2 0.6 fusion.25
  (53 shorter events, 0.9 us)
Async XLA Ops:
  2.3 1.6 %copy-start = (bf16[32,128,256]{2,1,0:T(8,128)(2,1)S(1)}, bf16[32,128,256]{2,1,0:T(8,128)(2,1)}, u32[]{:S(2)}) copy-start(bf16[32,128,256]{2,1,0:T(8,128)(2,1)} %frames_ref.1) | copy-start | bytes 6291460
  3.9 12.4 %copy-start.1 = (s32[2,256]{1,0:T(2,128)S(1)}, s32[2,256]{1,0:T(2,128)}, u32[]{:S(2)}) copy-start(s32[2,256]{1,0:T(2,128)} %param.7) | copy-start | bytes 6148
  3.9 12.4 %copy-start.2 = (s32[2,256]{1,0:T(2,128)S(1)}, s32[2,256]{1,0:T(2,128)}, u32[]{:S(2)}) copy-start(s32[2,256]{1,0:T(2,128)} %param.6) | copy-start | bytes 6148
  5.6 32.2 %collective-permute-start = (f32[12,32,256]{2,1,0:T(8,128)S(1)}, f32[12,32,256]{2,1,0:T(8,128)S(1)}, u32[]{:S(2)}, u32[]{:S(2)}) collective-permute-start(f32[12,32,256]{2,1,0:T(8,128)S(1)} %get-tuple-element.10), channel_id=1, source_target_pairs={{0,128},{128,256},{256,384},{384,0},{1,129},{129,257},{257,385},{3... | collective-permute-start | bytes 1179656 | tf_op jit(solution)/shard_map/ppermute | solution.py:240
  9.5 28.2 %collective-permute-start.1 = (f32[12,32,256]{2,1,0:T(8,128)S(1)}, f32[12,32,256]{2,1,0:T(8,128)S(1)}, u32[]{:S(2)}, u32[]{:S(2)}) collective-permute-start(f32[12,32,256]{2,1,0:T(8,128)S(1)} %get-tuple-element.11), channel_id=1, source_target_pairs={{0,384},{128,0},{256,128},{384,256},{1,385},{129,1},{257,129},{385... | collective-permute-start | bytes 1179656 | tf_op jit(solution)/shard_map/ppermute | solution.py:240
  12.7 25.1 %collective-permute-start.2 = (f32[12,32,256]{2,1,0:T(8,128)S(1)}, f32[12,32,256]{2,1,0:T(8,128)S(1)}, u32[]{:S(2)}, u32[]{:S(2)}) collective-permute-start(f32[12,32,256]{2,1,0:T(8,128)S(1)} %get-tuple-element.12), channel_id=1, source_target_pairs={{0,256},{128,384},{256,0},{384,128},{1,257},{129,385},{257,1},{385... | collective-permute-start | bytes 1179656 | tf_op jit(solution)/shard_map/ppermute | solution.py:240
  17.0 20.7 %all-to-all-start = ((s32[16,2,256]{2,1,0:T(2,128)}), s32[16,2,256]{2,1,0:T(2,128)S(1)}, u32[]{:S(2)}, u32[]{:S(2)}) async-start(s32[16,2,256]{2,1,0:T(2,128)} %broadcast_in_dim.148), calls=%async_computation | async-start | bytes 65536 | tf_op jit(solution)/shard_map/all_to_all | solution.py:186
  38.6 18.9 %all-to-all-start.1 = ((f32[16,6,4,128]{3,2,1,0:T(4,128)}), f32[16,6,4,128]{3,2,1,0:T(4,128)S(1)}, u32[]{:S(2)}, u32[]{:S(2)}) async-start(f32[16,6,4,128]{3,2,1,0:T(4,128)} %shard_map.47), calls=%async_computation.1 | async-start | bytes 393216 | tf_op jit(solution)/shard_map/all_to_all | solution.py:186
  57.7 5.8 %collective-permute-start.3 = (f32[3,4,3]{2,1,0:T(4,128)S(1)}, f32[3,4,3]{2,1,0:T(4,128)S(1)}, u32[]{:S(2)}, u32[]{:S(2)}) collective-permute-start(f32[3,4,3]{2,1,0:T(4,128)S(1)} %get-tuple-element.36), channel_id=1, source_target_pairs={{0,1},{1,2},{2,3},{3,4},{4,5},{5,6},{6,7},{7,0},{8,9},{9,10},{10,1... | collective-permute-start | bytes 440 | tf_op jit(solution)/shard_map/ppermute | solution.py:191
  62.7 3.1 %collective-permute-start.4 = (f32[3,4,3]{2,1,0:T(4,128)S(1)}, f32[3,4,3]{2,1,0:T(4,128)S(1)}, u32[]{:S(2)}, u32[]{:S(2)}) collective-permute-start(f32[3,4,3]{2,1,0:T(4,128)S(1)} %get-tuple-element.37), channel_id=1, source_target_pairs={{0,7},{1,0},{2,1},{3,2},{4,3},{5,4},{6,5},{7,6},{8,15},{9,8},{10,9... | collective-permute-start | bytes 440 | tf_op jit(solution)/shard_map/ppermute | solution.py:191
  65.9 9.5 %collective-permute-start.5 = (f32[3,3,262]{2,1,0:T(4,128)S(1)}, f32[3,3,262]{2,1,0:T(4,128)S(1)}, u32[]{:S(2)}, u32[]{:S(2)}) collective-permute-start(f32[3,3,262]{2,1,0:T(4,128)S(1)} %get-tuple-element.34), channel_id=1, source_target_pairs={{0,16},{8,24},{16,32},{24,40},{32,48},{40,56},{48,64},{56,72},{64,... | collective-permute-start | bytes 28304 | tf_op jit(solution)/shard_map/ppermute | solution.py:191
  68.2 8.1 %collective-permute-start.6 = (f32[3,3,262]{2,1,0:T(4,128)S(1)}, f32[3,3,262]{2,1,0:T(4,128)S(1)}, u32[]{:S(2)}, u32[]{:S(2)}) collective-permute-start(f32[3,3,262]{2,1,0:T(4,128)S(1)} %get-tuple-element.35), channel_id=1, source_target_pairs={{0,496},{8,504},{16,0},{24,8},{32,16},{40,24},{48,32},{56,40},{64,... | collective-permute-start | bytes 28304 | tf_op jit(solution)/shard_map/ppermute | solution.py:191
